TPU v7x, 128 devices: a whole 4x4x4 slice. The times are simulated.
128 devices in a mesh: pb: 8 (over x, core), pa: 16 (over z, y).
Axes of the slice: x: 4, y: 4, z: 4, core: 2. Of those that a mesh axis runs over, the one named last changes fastest.
Arguments:
- queries: bfloat16 [32768, 768], P('pb'), may hold values from -400 to 400
- passages: bfloat16 [65536, 768], P('pa'), may hold values from -400 to 400
- tiles: int32 [32, 8], replicated, may hold values from 0 to 63, as said below
- positives: int32 [32768], P('pb'), may hold values from 0 to 64511, as said below
- cotangent: float32 [32768], P('pb'), may hold values from -6 to 6
Outputs:
- losses: float32 [32768], P(('pb', 'pa'))
- query_grads: bfloat16 [32768, 768], P(('pb', 'pa'))
- passage_grads: bfloat16 [65536, 768], P('pa', 'pb')
Inputs may be any that keep to these rules, and one draw needn't show every extreme that they name: `tiles`: entries of one row are distinct; the first entry of row b is b * 2. `positives`: the positive of query i lies in passage block (i // 1024) * 2, the first tile of its query block.
All inputs are finite; a program needn't handle non-finite values.
Results may differ from a plain program's by a relative error of at most 0.015.
Values may be sent and summed in bfloat16 or wider, within the bound.
A program may use at most 128 MiB of HBM per device.

v0:
```python
import jax
import jax.numpy as jnp
from jax import lax
from jax.sharding import PartitionSpec as P

D = 768
BLK = 1024


def per_device(queries, passages, tiles, positives, cotangent):
    scale = D ** (-0.5)
    block_rows = BLK
    width = queries.shape[1]
    query_blocks = queries.shape[0] // block_rows
    passage_blocks = passages.shape[0] // block_rows
    listed = tiles.shape[1]
    row_index = lax.axis_index("pb")
    col_index = lax.axis_index("pa")
    mine = lax.dynamic_slice_in_dim(tiles, row_index * query_blocks, query_blocks, 0).reshape(-1)
    owned = mine // passage_blocks == col_index
    count = jnp.sum(owned.astype(jnp.int32))
    entries = mine.shape[0]
    ranking = jnp.where(owned, 0, entries).astype(jnp.int32) + jnp.arange(entries, dtype=jnp.int32)
    order = jnp.argsort(ranking)
    query_slot = order // listed
    passage_slot = mine[order] - col_index * passage_blocks
    pos_block = (positives // block_rows).reshape(query_blocks, block_rows)
    pos_col = (positives % block_rows).reshape(query_blocks, block_rows)
    weight_rows = cotangent.reshape(query_blocks, block_rows)
    columns = jnp.arange(block_rows, dtype=jnp.int32)

    def tile_scores(step):
        row_block = query_slot[step]
        col_block = passage_slot[step]
        query_tile = lax.dynamic_slice_in_dim(queries, row_block * block_rows, block_rows, 0)
        passage_tile = lax.dynamic_slice_in_dim(passages, col_block * block_rows, block_rows, 0)
        scores = (
            lax.dot_general(
                query_tile,
                passage_tile,
                (((1,), (1,)), ((), ())),
                preferred_element_type=jnp.float32,
            )
            * scale
        )
        global_block = col_block + col_index * passage_blocks
        target = (pos_block[row_block] == global_block)[:, None] & (
            columns[None, :] == pos_col[row_block][:, None]
        )
        return (row_block, col_block, query_tile, passage_tile, scores, target.astype(jnp.float32))

    def forward(step, carry):
        highs, totals, picked = carry
        row_block, col_block, query_tile, passage_tile, scores, target = tile_scores(step)
        before = highs[row_block]
        after = jnp.maximum(before, jnp.max(scores, axis=1))
        summed = totals[row_block] * jnp.exp(before - after) + jnp.sum(
            jnp.exp(scores - after[:, None]), axis=1
        )
        totals = totals.at[row_block].set(summed)
        highs = highs.at[row_block].set(after)
        picked = picked.at[row_block].add(jnp.sum(scores * target, axis=1))
        return (highs, totals, picked)

    start = (
        jnp.full((query_blocks, block_rows), -1e30, jnp.float32),
        jnp.zeros((query_blocks, block_rows), jnp.float32),
        jnp.zeros((query_blocks, block_rows), jnp.float32),
    )
    highs, totals, picked = lax.fori_loop(0, count, forward, start)
    peak = lax.pmax(highs, "pa")
    totals, picked = lax.psum((totals * jnp.exp(highs - peak), picked), "pa")
    highs = peak
    losses_all = (highs + jnp.log(totals) - picked).reshape(-1)
    share = queries.shape[0] // lax.axis_size("pa")
    losses = lax.dynamic_slice_in_dim(losses_all, col_index * share, share, 0)

    def backward(step, carry):
        query_acc, passage_acc = carry
        row_block, col_block, query_tile, passage_tile, scores, target = tile_scores(step)
        prob = jnp.exp(scores - highs[row_block][:, None]) / totals[row_block][:, None]
        grad = (weight_rows[row_block][:, None] * (prob - target) * scale).astype(jnp.bfloat16)
        query_term = jnp.dot(grad, passage_tile, preferred_element_type=jnp.float32)
        passage_term = lax.dot_general(
            grad, query_tile, (((0,), (0,)), ((), ())), preferred_element_type=jnp.float32
        )
        query_old = lax.dynamic_slice_in_dim(query_acc, row_block * block_rows, block_rows, 0)
        query_acc = lax.dynamic_update_slice_in_dim(
            query_acc, query_old + query_term, row_block * block_rows, 0
        )
        passage_old = lax.dynamic_slice_in_dim(passage_acc, col_block * block_rows, block_rows, 0)
        passage_acc = lax.dynamic_update_slice_in_dim(
            passage_acc, passage_old + passage_term, col_block * block_rows, 0
        )
        return (query_acc, passage_acc)

    begin = (
        jnp.zeros((queries.shape[0], width), jnp.float32),
        jnp.zeros((passages.shape[0], width), jnp.float32),
    )
    query_acc, passage_acc = lax.fori_loop(0, count, backward, begin)
    query_grads = lax.psum_scatter(
        query_acc.astype(jnp.bfloat16), "pa", scatter_dimension=0, tiled=True
    )
    passage_grads = lax.psum_scatter(
        passage_acc.astype(jnp.bfloat16), "pb", scatter_dimension=1, tiled=True
    )
    return (losses, query_grads, passage_grads)


def solution(mesh):
    in_specs = (P("pb", None), P("pa", None), P(), P("pb"), P("pb"))
    out_specs = (P(("pb", "pa")), P(("pb", "pa"), None), P("pa", "pb"))
    return jax.shard_map(
        per_device, mesh=mesh, in_specs=in_specs, out_specs=out_specs, check_vma=False
    )
```

profile of v0, /device:TPU:0, one launch (start us, length us, event | category | flops | bytes accessed | tf_op | source)
XLA Modules:
  0.0 607.8 jit_solution(1992865939345428778)
XLA Ops:
  12.7 58.4 %while.35 = (s32[]{:T(128)}, f32[4,1024]{1,0:T(4,128)S(1)}, f32[4,1024]{1,0:T(4,128)S(1)}, f32[4,1024]{1,0:T(4,128)S(1)}, s32[]{:T(128)}, /*index=5*/s32[32]{0:T...) while((s32[]{:T(128)}, f32[4,1024]{1,0:T(4,128)S(1)}, ...), condition=%wide.region_7.8_spmd.clone, body=%wide.region_2.7_spmd.clone.sunk | while | flops 1620058112 | bytes 11655612 | solution.py:70
  20.1 3.7 multiply_reduce_fusion.2
  63.4 3.7 multiply_reduce_fusion.2
  71.1 86.3 %pmax.7 = f32[4,1024]{1,0:T(4,128)S(1)} all-reduce(f32[4,1024]{1,0:T(4,128)S(1)} %get-tuple-element.370), channel_id=1, replica_groups=mesh['pb'=8,'pa'=16] {'pa'}, use_global_device_ids=true, to_apply=%region_8.9 | all-reduce | flops 4096 | bytes 32768 | tf_op jit(solution)/shard_map/pmax | solution.py:71
  157.4 69.6 %all-reduce = (f32[4,1024]{1,0:T(4,128)S(1)}, f32[4,1024]{1,0:T(4,128)S(1)}) all-reduce(f32[4,1024]{1,0:T(4,128)S(1)} %get-tuple-element.372, f32[4,1024]{1,0:T(4,128)S(1)} %exponential_multiply_fusion), channel_id=1, replica_groups=mesh['pb'=8,'pa'=16] {'pa'}, use_global_device_ids=true, to_apply=%region_10.11 | all-reduce | flops 8192 | bytes 65536 | tf_op jit(solution)/shard_map/psum | solution.py:72
  227.0 6.0 broadcast.119.clone
  233.0 5.4 broadcast.119
  238.4 135.3 %while.36 = (s32[]{:T(128)}, f32[4096,768]{1,0:T(8,128)}, f32[4096,768]{0,1:T(8,128)}, s32[]{:T(128)}, s32[32]{0:T(128)S(1)}, /*index=5*/f32[4,1024]{1,0:T(4,128...) while((s32[]{:T(128)}, f32[4096,768]{1,0:T(8,128)}, ...), condition=%wide.region_12.13_spmd.clone, body=%wide.region_11.12_spmd.clone.sunk | while | flops 4843897856 | bytes 58776012 | solution.py:101
  244.4 5.8 multiply_convert_fusion.2
  254.8 6.6 %convolution_add_fusion.2 = f32[1024,768]{1,0:T(8,128)} fusion(f32[1024,768]{1,0:T(8,128)} %copy.20, bf16[1024,1024]{1,0:T(8,128)(2,1)} %multiply_convert_fusion.2, bf16[4096,768]{1,0:T(8,128)(2,1)} %get-tuple-element.789, s32[]{:T(128)S(6)} %select_n.140), kind=kOutput, calls=%fused_computation.26.clone.1 | convolution fusion | flops 1611399168 | bytes 9961476 | tf_op jit(solution)/shard_map/while/body/dot_general | solution.py:84
  266.3 5.8 add_dynamic-update-slice_fusion.2
  278.0 5.8 multiply_convert_fusion.2
  288.4 6.6 %convolution_add_fusion.2 = f32[1024,768]{1,0:T(8,128)} fusion(f32[1024,768]{1,0:T(8,128)} %copy.20, bf16[1024,1024]{1,0:T(8,128)(2,1)} %multiply_convert_fusion.2, bf16[4096,768]{1,0:T(8,128)(2,1)} %get-tuple-element.789, s32[]{:T(128)S(6)} %select_n.140), kind=kOutput, calls=%fused_computation.26.clone.1 | convolution fusion | flops 1611399168 | bytes 9961476 | tf_op jit(solution)/shard_map/while/body/dot_general | solution.py:84
  299.9 5.8 add_dynamic-update-slice_fusion.2
  311.6 5.8 multiply_convert_fusion.2
  322.0 6.6 %convolution_add_fusion.2 = f32[1024,768]{1,0:T(8,128)} fusion(f32[1024,768]{1,0:T(8,128)} %copy.20, bf16[1024,1024]{1,0:T(8,128)(2,1)} %multiply_convert_fusion.2, bf16[4096,768]{1,0:T(8,128)(2,1)} %get-tuple-element.789, s32[]{:T(128)S(6)} %select_n.140), kind=kOutput, calls=%fused_computation.26.clone.1 | convolution fusion | flops 1611399168 | bytes 9961476 | tf_op jit(solution)/shard_map/while/body/dot_general | solution.py:84
  333.5 5.9 add_dynamic-update-slice_fusion.2
  345.2 5.8 multiply_convert_fusion.2
  355.6 6.6 %convolution_add_fusion.2 = f32[1024,768]{1,0:T(8,128)} fusion(f32[1024,768]{1,0:T(8,128)} %copy.20, bf16[1024,1024]{1,0:T(8,128)(2,1)} %multiply_convert_fusion.2, bf16[4096,768]{1,0:T(8,128)(2,1)} %get-tuple-element.789, s32[]{:T(128)S(6)} %select_n.140), kind=kOutput, calls=%fused_computation.26.clone.1 | convolution fusion | flops 1611399168 | bytes 9961476 | tf_op jit(solution)/shard_map/while/body/dot_general | solution.py:84
  367.2 5.9 add_dynamic-update-slice_fusion.2
  373.7 8.2 %convert_element_type.23 = bf16[4096,768]{0,1:T(8,128)(2,1)} convert(f32[4096,768]{0,1:T(8,128)} %get-tuple-element.374) | non-fusion elementwise | flops 3145728 | bytes 18874368 | tf_op jit(solution)/shard_map/convert_element_type | solution.py:106
  382.0 7.8 %convert_element_type.22 = bf16[4096,768]{1,0:T(8,128)(2,1)} convert(f32[4096,768]{1,0:T(8,128)} %get-tuple-element.373) | non-fusion elementwise | flops 3145728 | bytes 18874368 | tf_op jit(solution)/shard_map/convert_element_type | solution.py:103
  390.5 125.0 %reduce-scatter.5.cloned.1.call-done = bf16[4096,96]{0,1:T(8,128)(2,1)} async-done(((bf16[4096,768]{0,1:T(8,128)(2,1)}), bf16[4096,96]{0,1:T(8,128)(2,1)}) %reduce-scatter.5.cloned.1.call-update) | async-done | bytes 786448 | tf_op jit(solution)/shard_map/reduce_scatter | solution.py:105
  515.5 85.4 %reduce-scatter.3.cloned.1.call-done = bf16[256,768]{1,0:T(8,128)(2,1)} async-done(((bf16[4096,768]{1,0:T(8,128)(2,1)}), bf16[256,768]{1,0:T(8,128)(2,1)}) %reduce-scatter.3.cloned.1.call-update) | async-done | bytes 393232 | tf_op jit(solution)/shard_map/reduce_scatter | solution.py:102
  (123 shorter events, 80.6 us)
Async XLA Ops:
  7.2 508.4 %reduce-scatter.5.cloned.1.call-start = ((), (), s32[]{:S(2)}) async-start(), calls=%async_computation.3 | async-start | bytes 7077888 | tf_op jit(solution)/shard_map/reduce_scatter | solution.py:105
  263.8 2.5 copy-start
  297.4 2.5 copy-start
  331.0 2.5 copy-start
  364.6 2.5 copy-start
  382.0 219.0 %reduce-scatter.3.cloned.1.call-start = ((), (), s32[]{:S(2)}) async-start(), calls=%async_computation.2 | async-start | bytes 6684672 | tf_op jit(solution)/shard_map/reduce_scatter | solution.py:102
Sparse Core Ops, SparseCore 0:
  382.1 133.3 reduce-scatter.4
  519.5 81.3 reduce-scatter.2
where the time goes:
time: 610 us; the launch traced here: 608 us
  waiting for transfers between devices  210 us (34%)
  blocking collectives  156 us (26%)
  matrix products  88 us (14%)
  local copies, waits for them, and re-layouts  62.4 us (10%)
  loops' own time  38.7 us (6%)
  other arithmetic  38.1 us (6%)
  between operations  14.1 us (2%)
    reduce_scatter x1, waiting for transfers between devices, per_device(): lax.psum_scatter(passage_acc.astype(jnp.bfloat16), 'pb', scatter_dimensio...  125 us
    pmax x1, blocking collectives, per_device(): peak = lax.pmax(highs, 'pa')  86.3 us
    reduce_scatter x1, waiting for transfers between devices, per_device(): lax.psum_scatter(query_acc.astype(jnp.bfloat16), 'pa', scatter_dimension=...  85.4 us
    psum x1, blocking collectives, per_device(): totals, picked = lax.psum((totals * jnp.exp(highs - peak), picked), 'pa')  69.6 us
    dot_general x8, matrix products, tile_scores(): lax.dot_general(query_tile, passage_tile, (((1,), (1,)), ((), ())), prefe...  38.1 us
    dot_general x4, matrix products, backward(): lax.dot_general(grad, query_tile, (((0,), (0,)), ((), ())), preferred_ele...  26.5 us
    dot_general x4, matrix products, backward(): query_term = jnp.dot(grad, passage_tile, preferred_element_type=jnp.float32)  23.5 us
    another operation x1, loops' own time, per_device(): highs, totals, picked = lax.fori_loop(0, count, forward, start)  19.5 us
  transfers between devices with their start and end apart: 2, of which 2 were waited for; matrix products, arithmetic and copies ran while one was open for 1% of the time, Pallas kernels for 0%

commit v1 on v0

v1 whole, which is shorter than its diff:
```python
import jax
import jax.numpy as jnp
from jax import lax
from jax.experimental import pallas as pl
from jax.experimental.pallas import tpu as pltpu
from jax.sharding import PartitionSpec as P

D = 768
BLK = 1024
NB = 4
SCALE = D ** (-0.5)
LOG2E = 1.4426950408889634
CH = 256
F32 = jnp.float32
BF16 = jnp.bfloat16
LOW = -1e30


def listed(tiles_ref, group, owner, j):
    row = group * NB + j // NB
    block = owner * NB + j % NB
    hit = jnp.int32(0)
    for t in range(8):
        hit = hit | (tiles_ref[row, t] == block).astype(jnp.int32)
    return hit


def lane_iota(rows):
    return lax.broadcasted_iota(jnp.int32, (rows, 128), 1)


def column(x, lane):
    return jnp.sum(jnp.where(lane_iota(x.shape[0]) == lane, x, 0.0), axis=1, keepdims=True)


def forward_kernel(tiles_ref, rows_ref, q_hbm, p_hbm, e_hbm, m_ref, stats_ref,
                   q_v, p_v, e_v, t_v, cols_v, pick_v, q_sem, p_sem, e_sem):
    group = lax.axis_index("pb")
    owner = lax.axis_index("pa")
    q_copies = [pltpu.make_async_copy(q_hbm.at[pl.ds(b * BLK, BLK)], q_v.at[b], q_sem.at[b]) for b in range(NB)]
    p_copies = [pltpu.make_async_copy(p_hbm.at[pl.ds(b * BLK, BLK)], p_v.at[b], p_sem.at[b]) for b in range(NB)]
    for b in range(NB):
        p_copies[b].start()
        q_copies[b].start()
    m_ref[...] = jnp.full_like(m_ref, LOW)
    t_v[...] = jnp.zeros_like(t_v)
    pick_v[...] = jnp.zeros_like(pick_v)
    cols_v[...] = jnp.zeros_like(cols_v)
    cols_v[...] = jnp.concatenate([rows_ref[...], jnp.zeros((112, BLK), F32)], axis=0).T
    for b in range(NB):
        p_copies[b].wait()
        q_copies[b].wait()

    def store(slot, n):
        return pltpu.make_async_copy(e_v.at[slot], e_hbm.at[n], e_sem.at[slot])

    def step(j, n):
        hit = listed(tiles_ref, group, owner, j)

        @pl.when(hit == 1)
        def _():
            qb = j // NB
            pb = j % NB
            slot = n % 2

            @pl.when(n >= 2)
            def _():
                store(slot, 0).wait()

            first = (owner * NB + pb) == (group * NB + qb) * 2
            for c in range(BLK // CH):
                r = pl.ds(c * CH, CH)
                s = lax.dot_general(q_v[qb, r, :], p_v[pb], (((1,), (1,)), ((), ())), preferred_element_type=F32)
                top = jnp.max(s, axis=1, keepdims=True)
                e = jnp.exp2(s * (SCALE * LOG2E) - top * (SCALE * LOG2E))
                e_v[slot, r, :] = e.astype(BF16)
                here = lane_iota(CH) == j
                m_ref[r, :] = jnp.where(here, top * SCALE, m_ref[r, :])
                t_v[r, :] = jnp.where(here, jnp.sum(e, axis=1, keepdims=True), t_v[r, :])

                @pl.when(first)
                def _():
                    pos = column(cols_v[r, :], 4 + qb)
                    wide = lax.broadcasted_iota(jnp.int32, (CH, BLK), 1).astype(F32)
                    got = jnp.sum(jnp.where(wide == pos, s, 0.0), axis=1, keepdims=True) * SCALE
                    pick_v[r, :] = jnp.where(lane_iota(CH) == qb, got, pick_v[r, :])

            store(slot, n).start()

        return n + hit

    total = lax.fori_loop(0, NB * NB, step, jnp.int32(0))

    m_rows = m_ref[...].T
    t_rows = t_v[...].T
    pick_rows = pick_v[...].T
    highs, totals = [], []
    for b in range(NB):
        m4 = m_rows[b * NB : b * NB + NB, :]
        high = jnp.max(m4, axis=0, keepdims=True)
        highs.append(high)
        totals.append(jnp.sum(t_rows[b * NB : b * NB + NB, :] * jnp.exp(m4 - high), axis=0, keepdims=True))
    stats_ref[...] = jnp.concatenate(highs + totals + [pick_rows[0:8, :]], axis=0)

    @pl.when(total >= 1)
    def _():
        store((total - 1) % 2, 0).wait()

    @pl.when(total >= 2)
    def _():
        store(total % 2, 0).wait()


def backward_kernel(tiles_ref, rows_ref, m_ref, e_hbm, q_hbm, p_hbm, dq_ref, dp_ref,
                    q_v, qt_v, p_v, e_v, g_v, cols_v, dq_v, dp_v, q_sem, p_sem, e_sem):
    group = lax.axis_index("pb")
    owner = lax.axis_index("pa")
    p_copies = [pltpu.make_async_copy(p_hbm.at[pl.ds(b * BLK, BLK)], p_v.at[b], p_sem.at[b]) for b in range(NB)]
    q_copies = [pltpu.make_async_copy(q_hbm.at[pl.ds(b * BLK, BLK)], q_v.at[b], q_sem.at[b]) for b in range(NB)]
    for b in range(NB):
        p_copies[b].start()
        q_copies[b].start()

    def load(slot, n):
        return pltpu.make_async_copy(e_hbm.at[n], e_v.at[slot], e_sem.at[slot])

    count = lax.fori_loop(0, NB * NB, lambda j, n: n + listed(tiles_ref, group, owner, j), jnp.int32(0))

    @pl.when(count >= 1)
    def _():
        load(0, 0).start()

    cols_v[...] = jnp.concatenate([rows_ref[...], jnp.zeros((112, BLK), F32)], axis=0).T
    dp_v[...] = jnp.zeros_like(dp_v)
    for b in range(NB):
        p_copies[b].wait()
        q_copies[b].wait()

    def block(qb, n):
        qt_v[...] = q_v[qb].T
        dq_v[...] = jnp.zeros_like(dq_v)

        def step(pb, n):
            j = qb * NB + pb
            hit = listed(tiles_ref, group, owner, j)

            @pl.when(hit == 1)
            def _():
                slot = n % 2

                @pl.when(n + 1 < count)
                def _():
                    load(1 - slot, n + 1).start()

                load(slot, n).wait()
                first = (owner * NB + pb) == (group * NB + qb) * 2
                for c in range(BLK // CH):
                    r = pl.ds(c * CH, CH)
                    cols = cols_v[r, :]
                    ct = column(cols, 8 + qb) * SCALE
                    factor = ct * jnp.exp(column(m_ref[r, :], j) - column(cols, qb)) / column(cols, 4 + qb)
                    pos = jnp.where(first, column(cols, 12 + qb), -1.0)
                    wide = lax.broadcasted_iota(jnp.int32, (CH, BLK), 1).astype(F32)
                    g = e_v[slot, r, :].astype(F32) * factor - jnp.where(wide == pos, ct, 0.0)
                    g = g.astype(BF16)
                    g_v[r, :] = g
                    dq_v[r, :] += jnp.dot(g, p_v[pb], preferred_element_type=F32)
                for c in range(3):
                    r = pl.ds(c * CH, CH)
                    dp_v[pb, r, :] += jnp.dot(qt_v[r, :], g_v[...], preferred_element_type=F32)

            return n + hit

        n = lax.fori_loop(0, NB, step, n)
        dq_ref[pl.ds(qb * BLK, BLK), :] = dq_v[...].astype(BF16)
        return n

    lax.fori_loop(0, NB, block, jnp.int32(0))
    for b in range(NB):
        dp_ref[:, pl.ds(b * BLK, BLK)] = dp_v[b].astype(BF16)


SMEM = pl.BlockSpec(memory_space=pltpu.SMEM)
VMEM = pl.BlockSpec(memory_space=pltpu.VMEM)
ANY = pl.BlockSpec(memory_space=pl.ANY)


def forward(tiles, rows, queries, passages):
    return pl.pallas_call(
        forward_kernel,
        out_shape=[
            jax.ShapeDtypeStruct((NB * NB, BLK, BLK), BF16),
            jax.ShapeDtypeStruct((BLK, 128), F32),
            jax.ShapeDtypeStruct((16, BLK), F32),
        ],
        in_specs=[SMEM, VMEM, ANY, ANY],
        out_specs=[ANY, VMEM, VMEM],
        scratch_shapes=[
            pltpu.VMEM((NB, BLK, D), BF16),
            pltpu.VMEM((NB, BLK, D), BF16),
            pltpu.VMEM((2, BLK, BLK), BF16),
            pltpu.VMEM((BLK, 128), F32),
            pltpu.VMEM((BLK, 128), F32),
            pltpu.VMEM((BLK, 128), F32),
            pltpu.SemaphoreType.DMA((NB,)),
            pltpu.SemaphoreType.DMA((NB,)),
            pltpu.SemaphoreType.DMA((2,)),
        ],
        compiler_params=pltpu.CompilerParams(vmem_limit_bytes=56 * 2**20),
        name="forward",
    )(tiles, rows, queries, passages)


def backward(tiles, rows, m, e, queries, passages):
    return pl.pallas_call(
        backward_kernel,
        out_shape=[
            jax.ShapeDtypeStruct((NB * BLK, D), BF16),
            jax.ShapeDtypeStruct((D, NB * BLK), BF16),
        ],
        in_specs=[SMEM, VMEM, VMEM, ANY, ANY, ANY],
        out_specs=[VMEM, VMEM],
        scratch_shapes=[
            pltpu.VMEM((NB, BLK, D), BF16),
            pltpu.VMEM((D, BLK), BF16),
            pltpu.VMEM((NB, BLK, D), BF16),
            pltpu.VMEM((2, BLK, BLK), BF16),
            pltpu.VMEM((BLK, BLK), BF16),
            pltpu.VMEM((BLK, 128), F32),
            pltpu.VMEM((BLK, D), F32),
            pltpu.VMEM((NB, D, BLK), F32),
            pltpu.SemaphoreType.DMA((NB,)),
            pltpu.SemaphoreType.DMA((NB,)),
            pltpu.SemaphoreType.DMA((2,)),
        ],
        compiler_params=pltpu.CompilerParams(vmem_limit_bytes=60 * 2**20),
        name="backward",
    )(tiles, rows, m, e, queries, passages)


def per_device(queries, passages, tiles, positives, cotangent):
    col_index = lax.axis_index("pa")
    place = (positives % BLK).reshape(NB, BLK).astype(F32)
    weight = cotangent.reshape(NB, BLK)
    given = jnp.concatenate([weight, place, jnp.zeros((8, BLK), F32)], axis=0)
    e, m, stats = forward(tiles, given, queries, passages)
    peak = lax.pmax(stats[0:4], "pa")
    total, picked = lax.psum((stats[4:8] * jnp.exp(stats[0:4] - peak), stats[8:12]), "pa")
    losses_all = (peak + jnp.log(total) - picked).reshape(-1)
    share = NB * BLK // lax.axis_size("pa")
    losses = lax.dynamic_slice_in_dim(losses_all, col_index * share, share, 0)
    rows = jnp.concatenate([peak, total, weight, place], axis=0)
    dq, dp = backward(tiles, rows, m, e, queries, passages)
    query_grads = lax.psum_scatter(dq, "pa", scatter_dimension=0, tiled=True)
    passage_grads = lax.psum_scatter(dp, "pb", scatter_dimension=0, tiled=True).T
    return losses, query_grads, passage_grads


def solution(mesh):
    in_specs = (P("pb", None), P("pa", None), P(), P("pb"), P("pb"))
    out_specs = (P(("pb", "pa")), P(("pb", "pa"), None), P("pa", "pb"))
    return jax.shard_map(
        per_device, mesh=mesh, in_specs=in_specs, out_specs=out_specs, check_vma=False
    )
```

time: 610 us -> 352 us (0.58)
  matrix products: 88 us -> 0 us
  waiting for transfers between devices: 210 us -> 126 us
  Pallas kernels: 0 us -> 60.9 us
  local copies, waits for them, and re-layouts: 62.4 us -> 3.58 us
  loops' own time: 38.7 us -> 0 us
  other arithmetic: 38.1 us -> 2.95 us
  blocking collectives: 156 us -> 144 us
    dot_general x16 -> x0, matrix products: 88 us -> none  [the longest x8 38.1 us: tile_scores(): lax.dot_general(query_tile, passage_tile, (((1,), (1,)), ((), ())), prefe...]
    reduce_scatter x2, waiting for transfers between devices: 210 us -> 125 us  [the longest x1 80.6 us: per_device(): query_grads = lax.psum_scatter(dq, 'pa', scatter_dimension=0, tiled=True)]
    pallas_call x0 -> x2, Pallas kernels: none -> 60.9 us  [the longest x1 33.3 us: backward(): pl.pallas_call(backward_kernel, out_shape=[jax.ShapeDtypeStruct((NB * BLK...]
    another operation x2 -> x0, loops' own time: 38.7 us -> none  [the longest x1 19.5 us: per_device(): highs, totals, picked = lax.fori_loop(0, count, forward, start)]
    dynamic_slice x41 -> x0, local copies, waits for them, and re-layouts: 28.3 us -> none  [the longest x8 18.3 us: backward(): lax.dynamic_slice_in_dim(passage_acc, col_block * block_rows, block_rows, 0)]
    dynamic_update_slice x8 -> x0, local copies, waits for them, and re-layouts: 16.9 us -> none  [backward(): lax.dynamic_update_slice_in_dim(passage_acc, passage_old + passage_term,...]
    convert_element_type x2 -> x1, other arithmetic: 16 us -> 0.73 us  [per_device(): place = (positives % BLK).reshape(NB, BLK).astype(F32)]
    pmax x1, blocking collectives: 86.3 us -> 74.5 us  [per_device(): peak = lax.pmax(stats[0:4], 'pa')]
  transfers between devices with their start and end apart: 2 -> 2, of which waited for: 2 -> 2; matrix products, arithmetic and copies ran while one was open for 1% -> 0% of each run, Pallas kernels for 0% -> 0%
where the time goes in v1:
time: 352 us
  blocking collectives  144 us (41%)
  waiting for transfers between devices  126 us (36%)
  Pallas kernels  60.9 us (17%)
  between operations  14.1 us (4%)
  local copies, waits for them, and re-layouts  3.58 us (1%)
    reduce_scatter x1, waiting for transfers between devices, per_device(): query_grads = lax.psum_scatter(dq, 'pa', scatter_dimension=0, tiled=True)  80.6 us
    pmax x1, blocking collectives, per_device(): peak = lax.pmax(stats[0:4], 'pa')  74.5 us
    psum x1, blocking collectives, per_device(): lax.psum((stats[4:8] * jnp.exp(stats[0:4] - peak), stats[8:12]), 'pa')  69.6 us
    reduce_scatter x1, waiting for transfers between devices, per_device(): lax.psum_scatter(dp, 'pb', scatter_dimension=0, tiled=True)  44.6 us
    pallas_call x1, Pallas kernels, backward(): pl.pallas_call(backward_kernel, out_shape=[jax.ShapeDtypeStruct((NB * BLK...  33.3 us
    pallas_call x1, Pallas kernels, forward(): pl.pallas_call(forward_kernel, out_shape=[jax.ShapeDtypeStruct((NB * NB,...  27.6 us
  transfers between devices with their start and end apart: 2, of which 2 were waited for; matrix products, arithmetic and copies ran while one was open for 0% of the time, Pallas kernels for 0%

profile of v1, /device:TPU:0, one launch (start us, length us, event | category | flops | bytes accessed | tf_op | source)
XLA Modules:
  0.0 351.6 jit_solution(2800448732980829787)
XLA Ops:
  7.2 0.0 reduce-scatter.3.cloned.1.call-start
  7.2 1.4 copy.8.tiles_ref
  8.6 0.7 fusion.1
  9.3 0.7 reshape.14
  10.0 0.1 pad.6.clone
  10.1 0.7 maximum_maximum_fusion.rows_ref
  10.8 27.6 %forward.1 = (bf16[16,1024,1024]{2,1,0:T(8,128)(2,1)}, f32[1024,128]{1,0:T(8,128)}, f32[16,1024]{1,0:T(8,128)}) custom-call(s32[32,8]{1,0:T(8,128)} %copy.8.tiles_ref, f32[16,1024]{1,0:T(8,128)} %maximum_maximum_fusion.rows_ref, bf16[4096,768]{1,0:T(8,128)(2,1)} %q_hbm.3, bf16[4096,768]{1,0:T(8,128)(2,1)} %p_hbm.3), custom_call_target="tpu_custom_call" | custom-call | tf_op jit(solution)/shard_map/forward/pallas_call | solution.py:189
  38.4 0.8 slice.10
  39.2 74.5 %pmax.7 = f32[4,1024]{1,0:T(4,128)S(1)} all-reduce(f32[4,1024]{1,0:T(4,128)S(1)} %slice.10), channel_id=1, replica_groups=mesh['pb'=8,'pa'=16] {'pa'}, use_global_device_ids=true, to_apply=%region_0.1 | all-reduce | flops 4096 | bytes 32768 | tf_op jit(solution)/shard_map/pmax | solution.py:247
  113.7 0.8 exponential_multiply_fusion
  114.6 69.6 %all-reduce = (f32[4,1024]{1,0:T(4,128)S(1)}, f32[4,1024]{1,0:T(4,128)S(1)}) all-reduce(f32[4,1024]{1,0:T(4,128)S(1)} %get-tuple-element.16, f32[4,1024]{1,0:T(4,128)S(1)} %get-tuple-element.15), channel_id=1, replica_groups=mesh['pb'=8,'pa'=16] {'pa'}, use_global_device_ids=true, to_apply=%region_2.3 | all-reduce | flops 8192 | bytes 65536 | tf_op jit(solution)/shard_map/psum | solution.py:248
  184.1 0.6 pad_maximum_fusion.rows_ref
  184.8 33.3 %backward.1 = (bf16[4096,768]{1,0:T(8,128)(2,1)}, bf16[768,4096]{1,0:T(8,128)(2,1)}) custom-call(s32[32,8]{1,0:T(8,128)} %copy.8.tiles_ref, f32[16,1024]{1,0:T(8,128)} %pad_maximum_fusion.rows_ref, f32[1024,128]{1,0:T(8,128)} %get-tuple-element.9.m_ref, bf16[16,1024,1024]{2,1,0:T(8,128)(2,1)} %get-tuple-element.10.e_hbm, bf16[4096,768]{1,0:T(8,128)(2,1)} %q_hbm.3, ...), custom_call_target="tpu_custom_call" | custom-call | tf_op jit(solution)/shard_map/backward/pallas_call | solution.py:215
  218.1 0.0 reduce-scatter.3.cloned.1.call-update
  218.1 0.0 reduce-scatter.5.cloned.1.call-start
  218.1 0.7 reduce-scatter.5.cloned.1.call-update
  218.9 0.6 dynamic_slice.3
  219.5 80.6 %reduce-scatter.3.cloned.1.call-done = bf16[256,768]{1,0:T(8,128)(2,1)} async-done(((bf16[4096,768]{1,0:T(8,128)(2,1)}), bf16[256,768]{1,0:T(8,128)(2,1)}) %reduce-scatter.3.cloned.1.call-update) | async-done | bytes 393232 | tf_op jit(solution)/shard_map/reduce_scatter | solution.py:254
  300.1 44.6 %reduce-scatter.5.cloned.1.call-done = bf16[96,4096]{1,0:T(8,128)(2,1)} async-done(((bf16[768,4096]{1,0:T(8,128)(2,1)}), bf16[96,4096]{1,0:T(8,128)(2,1)}) %reduce-scatter.5.cloned.1.call-update) | async-done | bytes 786448 | tf_op jit(solution)/shard_map/reduce_scatter | solution.py:255
  (4 shorter events, 0.0 us)
Async XLA Ops:
  7.2 292.9 %reduce-scatter.3.cloned.1.call-start = ((), (), s32[]{:S(2)}) async-start(), calls=%async_computation.2 | async-start | bytes 6684672 | tf_op jit(solution)/shard_map/reduce_scatter | solution.py:254
  218.1 126.7 %reduce-scatter.5.cloned.1.call-start = ((), (), s32[]{:S(2)}) async-start(), calls=%async_computation.3 | async-start | bytes 7077888 | tf_op jit(solution)/shard_map/reduce_scatter | solution.py:255
Sparse Core Ops, SparseCore 0:
  218.2 81.8 reduce-scatter.2
  303.1 41.5 reduce-scatter.4

commit v2 on v1

--- a/solution.py
+++ b/solution.py
@@ -180,6 +180,161 @@
         dp_ref[:, pl.ds(b * BLK, BLK)] = dp_v[b].astype(BF16)
 
 
+def around():
+    group, owner = lax.axis_index("pb"), lax.axis_index("pa")
+    return group // 2, group % 2, owner // 4, owner % 4
+
+
+def device(x, core, z, y):
+    return (x * 2 + core, z * 4 + y)
+
+
+def greet(devices):
+    barrier = pltpu.get_barrier_semaphore()
+    for dev in devices:
+        pl.semaphore_signal(barrier, inc=1, device_id=dev, device_id_type=pl.DeviceIdType.MESH)
+    pl.semaphore_wait(barrier, len(devices))
+
+
+def remote(src, dst, send_sem, recv_sem, dev):
+    return pltpu.make_async_remote_copy(
+        src_ref=src, dst_ref=dst, send_sem=send_sem, recv_sem=recv_sem,
+        device_id=dev, device_id_type=pl.DeviceIdType.MESH)
+
+
+def stats_kernel(rows_ref, out_ref, losses_ref, now, buf, send_sem, recv_sem):
+    x, core, z, y = around()
+    peers = [[device(x, core, (z + d) % 4, y) for d in (1, 2, 3)], [device(x, core, z, (y + d) % 4) for d in (1, 2, 3)]]
+    greet(peers[0] + peers[1])
+    now[0] = rows_ref[...]
+    for stage in range(2):
+        copies = [
+            remote(now.at[stage], buf.at[stage, d], send_sem.at[stage, d], recv_sem.at[stage, d], peers[stage][d])
+            for d in range(3)
+        ]
+        for c in copies:
+            c.start()
+        for c in copies:
+            c.wait()
+        parts = [now[stage]] + [buf[stage, d] for d in range(3)]
+        high = parts[0][0:4]
+        for p in parts[1:]:
+            high = jnp.maximum(high, p[0:4])
+        total = sum(p[4:8] * jnp.exp(p[0:4] - high) for p in parts)
+        rest = sum(p[8:16] for p in parts)
+        now[stage + 1] = jnp.concatenate([high, total, rest], axis=0)
+    out_ref[...] = now[2]
+    span = pl.ds(pl.multiple_of(y * 256, 256), 256)
+    losses_ref[...] = now[2, pl.ds(z, 1), span] + jnp.log(now[2, pl.ds(4 + z, 1), span]) - now[2, pl.ds(8 + z, 1), span]
+
+
+AHEAD, RAW, SUMMED = 0, 1, 2
+
+
+class Ring:
+    def __init__(self, me, chunk, neighbours, buf, acc, send_sem, recv_sem):
+        self.me, self.chunk, self.buf, self.acc = me, chunk, buf, acc
+        self.send = lambda d, kind, src: remote(
+            src, buf.at[d, kind], send_sem.at[d, kind], recv_sem.at[d, kind], neighbours[d])
+        self.sent = {}
+
+    def at(self, step, half):
+        return self.chunk((self.me + step) % 4, half)
+
+    def go(self, d, kind, src):
+        c = self.send(d, kind, src)
+        c.start()
+        self.sent[d, kind] = c
+
+    def ahead(self):
+        self.go(0, AHEAD, self.at(2, 0))
+        self.go(1, AHEAD, self.at(2, 1))
+
+    def raw(self):
+        self.go(0, RAW, self.at(1, 1))
+        self.go(1, RAW, self.at(3, 0))
+
+    def forward(self):
+        for d, step in ((0, 1), (1, 3)):
+            self.sent[d, AHEAD].wait_recv()
+            self.acc[d] = (self.at(step, d)[...].astype(F32) + self.buf[d, AHEAD].astype(F32)).astype(BF16)
+            self.go(d, SUMMED, self.acc.at[d])
+
+    def result(self, half):
+        a, b = (SUMMED, RAW) if half == 0 else (RAW, SUMMED)
+        self.sent[0, a].wait_recv()
+        self.sent[1, b].wait_recv()
+        return self.at(0, half)[...].astype(F32) + self.buf[0, a].astype(F32) + self.buf[1, b].astype(F32)
+
+    def drain(self):
+        for c in self.sent.values():
+            c.wait_send()
+
+
+def scatter_kernel(dq_ref, dp_ref, qg_ref, pg_ref,
+                   a1_buf, a1_acc, a1_sum, b1_buf, b1_acc, b1_sum, a2_buf, a2_acc, b2_buf, b2_acc,
+                   x_buf, x_acc, x_sum, core_buf, ssem, rsem, core_ssem, core_rsem):
+    x, core, z, y = around()
+    z_next = [device(x, core, (z + 1) % 4, y), device(x, core, (z + 3) % 4, y)]
+    y_next = [device(x, core, z, (y + 1) % 4), device(x, core, z, (y + 3) % 4)]
+    x_next = [device((x + 1) % 4, core, z, y), device((x + 3) % 4, core, z, y)]
+    mate = device(x, 1 - core, z, y)
+    greet(z_next + y_next + x_next + [mate])
+    left, right = pl.ds(0, 384), pl.ds(384, 384)
+    a1 = Ring(z, lambda j, h: dq_ref.at[j, pl.ds(2 * h, 2), :, left], z_next, a1_buf, a1_acc, ssem.at[0], rsem.at[0])
+    b1 = Ring(y, lambda j, h: dq_ref.at[pl.ds(2 * h, 2), j, :, right], y_next, b1_buf, b1_acc, ssem.at[1], rsem.at[1])
+    a2 = Ring(y, lambda j, h: a1_sum.at[j, pl.ds(128 * h, 128)], y_next, a2_buf, a2_acc, ssem.at[2], rsem.at[2])
+    b2 = Ring(z, lambda j, h: b1_sum.at[j, pl.ds(128 * h, 128)], z_next, b2_buf, b2_acc, ssem.at[3], rsem.at[3])
+    xr = Ring(x, lambda j, h: x_sum.at[j, h], x_next, x_buf, x_acc, ssem.at[4], rsem.at[4])
+    cores = []
+    for k, step in enumerate((2, 1, 3, 0)):
+        place = (x + step) % 4
+        cores.append(remote(dp_ref.at[place, 1 - core], core_buf.at[k], core_ssem.at[k], core_rsem.at[k], mate))
+    cores[0].start()
+    a1.ahead()
+    b1.ahead()
+    cores[1].start()
+    a1.raw()
+    b1.raw()
+    cores[2].start()
+    cores[3].start()
+
+    def add_core(k, step):
+        place = (x + step) % 4
+        cores[k].wait_recv()
+        for h in range(2):
+            x_sum[place, h] = (dp_ref[place, core, h].astype(F32) + core_buf[k, h].astype(F32)).astype(BF16)
+
+    add_core(0, 2)
+    xr.ahead()
+    add_core(1, 1)
+    add_core(2, 3)
+    xr.raw()
+    add_core(3, 0)
+    a1.forward()
+    b1.forward()
+    xr.forward()
+    for h in range(2):
+        a1_sum[pl.ds(2 * h, 2)] = a1.result(h).astype(BF16)
+    a2.ahead()
+    a2.raw()
+    for h in range(2):
+        b1_sum[pl.ds(2 * h, 2)] = b1.result(h).astype(BF16)
+    b2.ahead()
+    b2.raw()
+    a2.forward()
+    b2.forward()
+    for h in range(2):
+        pg_ref[pl.ds(48 * h, 48), :] = xr.result(h)
+    for h in range(2):
+        qg_ref[pl.ds(128 * h, 128), left] = a2.result(h).astype(BF16)
+        qg_ref[pl.ds(128 * h, 128), right] = b2.result(h).astype(BF16)
+    for ring in (a1, b1, a2, b2, xr):
+        ring.drain()
+    for c in cores:
+        c.wait_send()
+
+
 SMEM = pl.BlockSpec(memory_space=pltpu.SMEM)
 VMEM = pl.BlockSpec(memory_space=pltpu.VMEM)
 ANY = pl.BlockSpec(memory_space=pl.ANY)
@@ -238,22 +393,57 @@
     )(tiles, rows, m, e, queries, passages)
 
 
+def combine(rows):
+    return pl.pallas_call(
+        stats_kernel,
+        out_shape=[jax.ShapeDtypeStruct((16, BLK), F32), jax.ShapeDtypeStruct((1, 256), F32)],
+        in_specs=[VMEM],
+        out_specs=[VMEM, VMEM],
+        scratch_shapes=[
+            pltpu.VMEM((3, 16, BLK), F32),
+            pltpu.VMEM((2, 3, 16, BLK), F32),
+            pltpu.SemaphoreType.DMA((2, 3)),
+            pltpu.SemaphoreType.DMA((2, 3)),
+        ],
+        compiler_params=pltpu.CompilerParams(collective_id=1, has_side_effects=True),
+        name="combine",
+    )(rows)
+
+
+def scatter(dq, dp):
+    big, small = (2, 3, 2, 256, 384), (2, 3, 128, 384)
+    return pl.pallas_call(
+        scatter_kernel,
+        out_shape=[jax.ShapeDtypeStruct((256, D), BF16), jax.ShapeDtypeStruct((96, NB * BLK), F32)],
+        in_specs=[VMEM, VMEM],
+        out_specs=[VMEM, VMEM],
+        scratch_shapes=[
+            pltpu.VMEM(big, BF16), pltpu.VMEM((2, 2, 256, 384), BF16), pltpu.VMEM((4, 256, 384), BF16),
+            pltpu.VMEM(big, BF16), pltpu.VMEM((2, 2, 256, 384), BF16), pltpu.VMEM((4, 256, 384), BF16),
+            pltpu.VMEM(small, BF16), pltpu.VMEM((2, 128, 384), BF16),
+            pltpu.VMEM(small, BF16), pltpu.VMEM((2, 128, 384), BF16),
+            pltpu.VMEM((2, 3, 48, NB * BLK), BF16), pltpu.VMEM((2, 48, NB * BLK), BF16),
+            pltpu.VMEM((4, 2, 48, NB * BLK), BF16),
+            pltpu.VMEM((4, 2, 48, NB * BLK), BF16),
+            pltpu.SemaphoreType.DMA((5, 2, 3)), pltpu.SemaphoreType.DMA((5, 2, 3)),
+            pltpu.SemaphoreType.DMA((4,)), pltpu.SemaphoreType.DMA((4,)),
+        ],
+        compiler_params=pltpu.CompilerParams(
+            collective_id=2, has_side_effects=True, vmem_limit_bytes=56 * 2**20),
+        name="scatter",
+    )(dq.reshape(4, 4, 256, D), dp.reshape(4, 2, 2, 48, NB * BLK))
+
+
 def per_device(queries, passages, tiles, positives, cotangent):
-    col_index = lax.axis_index("pa")
     place = (positives % BLK).reshape(NB, BLK).astype(F32)
     weight = cotangent.reshape(NB, BLK)
     given = jnp.concatenate([weight, place, jnp.zeros((8, BLK), F32)], axis=0)
     e, m, stats = forward(tiles, given, queries, passages)
-    peak = lax.pmax(stats[0:4], "pa")
-    total, picked = lax.psum((stats[4:8] * jnp.exp(stats[0:4] - peak), stats[8:12]), "pa")
-    losses_all = (peak + jnp.log(total) - picked).reshape(-1)
-    share = NB * BLK // lax.axis_size("pa")
-    losses = lax.dynamic_slice_in_dim(losses_all, col_index * share, share, 0)
-    rows = jnp.concatenate([peak, total, weight, place], axis=0)
+    stats, losses = combine(stats)
+    rows = jnp.concatenate([stats[0:8], weight, place], axis=0)
     dq, dp = backward(tiles, rows, m, e, queries, passages)
-    query_grads = lax.psum_scatter(dq, "pa", scatter_dimension=0, tiled=True)
-    passage_grads = lax.psum_scatter(dp, "pb", scatter_dimension=0, tiled=True).T
-    return losses, query_grads, passage_grads
+    query_grads, passage_grads = scatter(dq, dp)
+    return losses.reshape(256), query_grads, passage_grads.T.astype(BF16)
 
 
 def solution(mesh):

time: 352 us -> 149 us (0.42)
  blocking collectives: 144 us -> 0 us
  waiting for transfers between devices: 126 us -> 0 us
  Pallas kernels: 60.9 us -> 137 us
  between operations: 14.1 us -> 0.69 us
    reduce_scatter x2 -> x0, waiting for transfers between devices: 125 us -> none  [the longest x1 80.6 us: per_device(): query_grads = lax.psum_scatter(dq, 'pa', scatter_dimension=0, tiled=True)]
    pallas_call x0 -> x2, Pallas kernels: none -> 76.5 us  [the longest x1 58.1 us: scatter(): pl.pallas_call(scatter_kernel, out_shape=[jax.ShapeDtypeStruct((256, D),...]
    pmax x1 -> x0, blocking collectives: 74.5 us -> none  [per_device(): peak = lax.pmax(stats[0:4], 'pa')]
    psum x1 -> x0, blocking collectives: 69.6 us -> none  [per_device(): lax.psum((stats[4:8] * jnp.exp(stats[0:4] - peak), stats[8:12]), 'pa')]
  transfers between devices with their start and end apart: 2 -> 0, of which waited for: 2 -> 0; matrix products, arithmetic and copies ran while one was open for 0% -> 0% of each run, Pallas kernels for 0% -> 0%
where the time goes in v2:
time: 149 us; the launch traced here: 148 us
  Pallas kernels  137 us (92%)
  local copies, waits for them, and re-layouts  5.27 us (4%)
  other arithmetic  4.45 us (3%)
    pallas_call x1, Pallas kernels, scatter(): pl.pallas_call(scatter_kernel, out_shape=[jax.ShapeDtypeStruct((256, D),...  58.1 us
    pallas_call x1, Pallas kernels, backward(): pl.pallas_call(backward_kernel, out_shape=[jax.ShapeDtypeStruct((NB * BLK...  33.5 us
    pallas_call x1, Pallas kernels, forward(): pl.pallas_call(forward_kernel, out_shape=[jax.ShapeDtypeStruct((NB * NB,...  27.5 us
    pallas_call x1, Pallas kernels, combine(): pl.pallas_call(stats_kernel, out_shape=[jax.ShapeDtypeStruct((16, BLK), F...  18.4 us
    unnamed x5, local copies, waits for them, and re-layouts  3.69 us

profile of v2, /device:TPU:0, one launch (start us, length us, event | category | flops | bytes accessed | tf_op | source)
XLA Modules:
  0.0 147.8 jit_solution(7818234148626536482)
XLA Ops:
  0.6 0.1 pad.5.clone
  0.7 1.4 copy.8.tiles_ref
  2.1 0.7 reshape.20
  2.8 0.7 fusion.1
  3.5 0.7 maximum_maximum_fusion.rows_ref
  4.2 27.5 %forward.1 = (bf16[16,1024,1024]{2,1,0:T(8,128)(2,1)}, f32[1024,128]{1,0:T(8,128)}, f32[16,1024]{1,0:T(8,128)}) custom-call(s32[32,8]{1,0:T(8,128)} %copy.8.tiles_ref, f32[16,1024]{1,0:T(8,128)} %maximum_maximum_fusion.rows_ref, bf16[4096,768]{1,0:T(8,128)(2,1)} %q_hbm.3, bf16[4096,768]{1,0:T(8,128)(2,1)} %p_hbm.3), custom_call_target="tpu_custom_call" | custom-call | tf_op jit(solution)/shard_map/forward/pallas_call | solution.py:344
  31.7 18.4 %combine.1 = (f32[16,1024]{1,0:T(8,128)}, f32[1,256]{1,0:T(1,128)}) custom-call(f32[16,1024]{1,0:T(8,128)} %get-tuple-element.12.rows_ref), custom_call_target="tpu_custom_call" | custom-call | tf_op jit(solution)/shard_map/combine/pallas_call | solution.py:397
  50.1 0.8 slice.3
  50.8 0.6 pad_maximum_fusion.rows_ref
  51.5 33.5 %backward.1 = (bf16[4096,768]{1,0:T(8,128)(2,1)}, bf16[768,4096]{1,0:T(8,128)(2,1)}) custom-call(s32[32,8]{1,0:T(8,128)} %copy.8.tiles_ref, f32[16,1024]{1,0:T(8,128)} %pad_maximum_fusion.rows_ref, f32[1024,128]{1,0:T(8,128)} %get-tuple-element.15.m_ref, bf16[16,1024,1024]{2,1,0:T(8,128)(2,1)} %get-tuple-element.16.e_hbm, bf16[4096,768]{1,0:T(8,128)(2,1)} %q_hbm.3, ...), custom_call_target="tpu_custom_call" | custom-call | tf_op jit(solution)/shard_map/backward/pallas_call | solution.py:370
  85.0 0.0 copy-start
  85.0 58.1 %scatter.1 = (bf16[256,768]{1,0:T(8,128)(2,1)}, f32[96,4096]{1,0:T(8,128)}) custom-call(bf16[4,4,256,768]{3,2,1,0:T(8,128)(2,1)} %bitcast.5, bf16[4,2,2,48,4096]{4,3,2,1,0:T(8,128)(2,1)} %bitcast.6), custom_call_target="tpu_custom_call" | custom-call | tf_op jit(solution)/shard_map/scatter/pallas_call | solution.py:415
  143.1 2.4 %convert_bitcast_fusion = bf16[4096,96]{0,1:T(8,128)(2,1)} fusion(f32[96,4096]{1,0:T(8,128)} %get-tuple-element.20), kind=kLoop, calls=%fused_computation | loop fusion | flops 393216 | bytes 2359296 | tf_op jit(solution)/shard_map/convert_element_type | solution.py:446
  145.5 0.0 copy-done
  145.5 0.6 copy.12
  146.0 1.8 %copy.13 = bf16[256,768]{1,0:T(8,128)(2,1)} copy(bf16[256,768]{1,0:T(8,128)(2,1)} %get-tuple-element.25) | data formatting | bytes 786432
  (2 shorter events, 0.0 us)
Async XLA Ops:
  85.0 60.5 %copy-start = (f32[1,256]{1,0:T(1,128)S(1)}, f32[1,256]{1,0:T(1,128)}, u32[]{:S(2)}) copy-start(f32[1,256]{1,0:T(1,128)} %get-tuple-element.13) | copy-start | bytes 3076

commit v3 on v2

v3 whole, which is shorter than its diff:
```python
import jax
import jax.numpy as jnp
from jax import lax
from jax.experimental import pallas as pl
from jax.experimental.pallas import tpu as pltpu
from jax.sharding import PartitionSpec as P

D = 768
BLK = 1024
NB = 4
LISTED = 8
SL = 64
SCALE = D ** (-0.5)
LOG2E = 1.4426950408889634
CH = 256
F32 = jnp.float32
BF16 = jnp.bfloat16


def around():
    group, owner = lax.axis_index("pb"), lax.axis_index("pa")
    return group // 2, group % 2, owner // 4, owner % 4


def device(x, core, z, y):
    return (x * 2 + core, z * 4 + y)


def greet(devices):
    barrier = pltpu.get_barrier_semaphore()
    for dev in devices:
        pl.semaphore_signal(barrier, inc=1, device_id=dev, device_id_type=pl.DeviceIdType.MESH)
    pl.semaphore_wait(barrier, len(devices))


def remote(src, dst, send_sem, recv_sem, dev):
    return pltpu.make_async_remote_copy(
        src_ref=src, dst_ref=dst, send_sem=send_sem, recv_sem=recv_sem,
        device_id=dev, device_id_type=pl.DeviceIdType.MESH)


def stats_kernel(rows_ref, out_ref, losses_ref, now, buf, send_sem, recv_sem):
    x, core, z, y = around()
    peers = [[device(x, core, (z + d) % 4, y) for d in (1, 2, 3)], [device(x, core, z, (y + d) % 4) for d in (1, 2, 3)]]
    greet(peers[0] + peers[1])
    now[0] = rows_ref[...]
    for stage in range(2):
        copies = [
            remote(now.at[stage], buf.at[stage, d], send_sem.at[stage, d], recv_sem.at[stage, d], peers[stage][d])
            for d in range(3)
        ]
        for c in copies:
            c.start()
        for c in copies:
            c.wait()
        parts = [now[stage]] + [buf[stage, d] for d in range(3)]
        high = parts[0][0:4]
        for p in parts[1:]:
            high = jnp.maximum(high, p[0:4])
        total = sum(p[4:8] * jnp.exp(p[0:4] - high) for p in parts)
        rest = sum(p[8:16] for p in parts)
        now[stage + 1] = jnp.concatenate([high, total, rest], axis=0)
    out_ref[...] = now[2]
    span = pl.ds(pl.multiple_of(y * 256, 256), 256)
    losses_ref[...] = now[2, pl.ds(z, 1), span] + jnp.log(now[2, pl.ds(4 + z, 1), span]) - now[2, pl.ds(8 + z, 1), span]


AHEAD, RAW, SUMMED = 0, 1, 2


class Ring:
    def __init__(self, me, chunk, neighbours, buf, acc, send_sem, recv_sem):
        self.me, self.chunk, self.buf, self.acc = me, chunk, buf, acc
        self.send = lambda d, kind, src: remote(
            src, buf.at[d, kind], send_sem.at[d, kind], recv_sem.at[d, kind], neighbours[d])
        self.sent = {}

    def at(self, step, half):
        return self.chunk((self.me + step) % 4, half)

    def go(self, d, kind, src):
        c = self.send(d, kind, src)
        c.start()
        self.sent[d, kind] = c

    def ahead(self):
        self.go(0, AHEAD, self.at(2, 0))
        self.go(1, AHEAD, self.at(2, 1))

    def raw(self):
        self.go(0, RAW, self.at(1, 1))
        self.go(1, RAW, self.at(3, 0))

    def forward(self):
        for d, step in ((0, 1), (1, 3)):
            self.sent[d, AHEAD].wait_recv()
            self.acc[d] = (self.at(step, d)[...].astype(F32) + self.buf[d, AHEAD].astype(F32)).astype(BF16)
            self.go(d, SUMMED, self.acc.at[d])

    def result(self, half):
        a, b = (SUMMED, RAW) if half == 0 else (RAW, SUMMED)
        self.sent[0, a].wait_recv()
        self.sent[1, b].wait_recv()
        return self.at(0, half)[...].astype(F32) + self.buf[0, a].astype(F32) + self.buf[1, b].astype(F32)

    def drain(self):
        for c in self.sent.values():
            c.wait_send()


def distribute_kernel(p_hbm, sel_hbm, own_sem, ssem, rsem, mate_ssem, mate_rsem, x_ssem, x_rsem, fwd_ssem, fwd_rsem):
    x, core, z, y = around()
    me = z * 4 + y
    mate = device(x, 1 - core, z, y)
    to = (x + 1 + 2 * core) % 4
    source = (x + 3 + 2 * core) % 4
    x_to, x_from = device(to, core, z, y), device(source, core, z, y)
    peers = [(dz, dy) for dz in (0, 2, 1, 3) for dy in (2, 1, 3, 0) if dz or dy]
    place = {k: ((z + k[0]) % 4, (y + k[1]) % 4) for k in peers}
    greet([device(x, core, *place[k]) for k in peers] + [mate, x_to, x_from])
    mine = (x + core) % 4
    theirs = (source + core) % 4
    own = pltpu.make_async_copy(p_hbm.at[mine, me], sel_hbm.at[mine, me], own_sem)
    own.start()
    sends = []
    for k in peers:
        tz, ty = place[k]
        c = remote(p_hbm.at[mine, tz * 4 + ty], sel_hbm.at[mine, me], ssem.at[tz * 4 + ty], rsem.at[me],
                   device(x, core, tz, ty))
        c.start()
        sends.append(c)
    hands = []
    own.wait()

    def group(b, zz):
        return sel_hbm.at[b, pl.ds(zz * 4, 4)]

    order = [(z + dz) % 4 for dz in (0, 2, 3, 1)]
    for n, zz in enumerate(order):
        for dy in range(4):
            if n == 0 and dy == 0:
                continue
            yy = (y + dy) % 4
            remote(p_hbm.at[mine, me], sel_hbm.at[mine, zz * 4 + yy], ssem.at[me], rsem.at[zz * 4 + yy],
                   device(x, core, zz, yy)).wait_recv()
        for a, b, dev in ((x_ssem, x_rsem, x_to), (mate_ssem, mate_rsem, mate)):
            c = remote(group(mine, zz), group(mine, zz), a.at[n], b.at[n], dev)
            c.start()
            hands.append(c)
    for n, zz in enumerate(order):
        remote(group(mine, zz), group(theirs, zz), x_ssem.at[n], x_rsem.at[n], x_from).wait_recv()
        c = remote(group(theirs, zz), group(theirs, zz), fwd_ssem.at[n], fwd_rsem.at[n], mate)
        c.start()
        hands.append(c)
    for n, zz in enumerate(order):
        for a, b in ((mate_ssem, mate_rsem), (fwd_ssem, fwd_rsem)):
            remote(group(mine, zz), group(mine, zz), a.at[n], b.at[n], mate).wait_recv()
    for c in sends + hands:
        c.wait_send()


def forward_kernel(tiles_ref, rows_ref, q_hbm, sel_hbm, e_ref, pq_ref, stats_ref, q_v, sel_v, q_sem, sel_sem):
    group = lax.axis_index("pb")
    owner = lax.axis_index("pa")
    sel_copy = pltpu.make_async_copy(sel_hbm, sel_v, sel_sem)
    sel_copy.start()
    q_copies = [pltpu.make_async_copy(q_hbm.at[b], q_v.at[b], q_sem.at[b]) for b in range(NB)]
    for c in q_copies:
        c.start()
    sel_copy.wait()
    for b in range(NB):
        for t in range(LISTED):
            block = tiles_ref[group * NB + b, t]
            pq_ref[b, pl.ds(t * SL, SL), :] = sel_v[block % NB, block // NB]
        q_copies[b].wait()
        for c in range(BLK // CH):
            r = pl.ds(c * CH, CH)
            s = lax.dot_general(pq_ref[b], q_v[b, r, :], (((1,), (1,)), ((), ())), preferred_element_type=F32)
            top = jnp.max(s, axis=0, keepdims=True)
            e = jnp.exp2(s * (SCALE * LOG2E) - top * (SCALE * LOG2E))
            e_ref[b, :, r] = e.astype(BF16)
            stats_ref[b : b + 1, r] = top * SCALE
            stats_ref[NB + b : NB + b + 1, r] = jnp.sum(e, axis=0, keepdims=True)
            pos = rows_ref[NB + b : NB + b + 1, r] - (owner * SL).astype(F32)
            at = lax.broadcasted_iota(jnp.int32, (SL, CH), 0).astype(F32) == pos
            stats_ref[2 * NB + b : 2 * NB + b + 1, r] = (
                jnp.sum(jnp.where(at, s[0:SL], 0.0), axis=0, keepdims=True) * SCALE)
    stats_ref[12:16, :] = jnp.zeros((4, BLK), F32)


def backward_kernel(tiles_ref, rows_ref, m_ref, all_ref, e_ref, pq_ref, q_ref, dq_ref, dp_ref, part_v, slot_s):
    group = lax.axis_index("pb")
    owner = lax.axis_index("pa")
    for b in range(NB):
        part_v[b, LISTED] = jnp.zeros((SL, D), F32)

        def clear(p, carry, b=b):
            slot_s[b, p] = LISTED
            return carry

        lax.fori_loop(0, 64, clear, 0)
        for t in range(LISTED):
            slot_s[b, tiles_ref[group * NB + b, t]] = t
    for b in range(NB):
        one = slice(b, b + 1)
        weight = rows_ref[one, :] * SCALE
        factor = weight * jnp.exp(m_ref[one, :] - all_ref[one, :]) / all_ref[NB + b : NB + b + 1, :]
        pos = rows_ref[NB + b : NB + b + 1, :] - (owner * SL).astype(F32)
        at = lax.broadcasted_iota(jnp.int32, (SL, BLK), 0).astype(F32) == pos
        g0 = (e_ref[b, 0:SL, :].astype(F32) * factor - jnp.where(at, weight, 0.0)).astype(BF16)
        g1 = (e_ref[b, SL:, :].astype(F32) * factor).astype(BF16)
        g = jnp.concatenate([g0, g1], axis=0)
        dq_ref[b] = lax.dot_general(
            g, pq_ref[b], (((0,), (0,)), ((), ())), preferred_element_type=F32).astype(BF16)
        part_v[b, 0:LISTED] = jnp.dot(g, q_ref[b], preferred_element_type=F32).reshape(LISTED, SL, D)

    def dense(n, carry):
        rows = []
        for k in range(4):
            p = n * 4 + k
            rows.append(sum(part_v[b, slot_s[b, p]] for b in range(NB)))
        dp_ref[:, pl.ds(pl.multiple_of(n * 256, 256), 256)] = jnp.concatenate(rows, axis=0).astype(BF16).T
        return carry

    lax.fori_loop(0, 16, dense, 0)


def scatter_kernel(dq_ref, dp_ref, qg_ref, pg_ref,
                   a1_buf, a1_acc, a1_sum, b1_buf, b1_acc, b1_sum, a2_buf, a2_acc, b2_buf, b2_acc,
                   x_buf, x_acc, x_sum, core_buf, back, got, ssem, rsem, core_ssem, core_rsem, back_ssem, back_rsem):
    x, core, z, y = around()
    z_next = [device(x, core, (z + 1) % 4, y), device(x, core, (z + 3) % 4, y)]
    y_next = [device(x, core, z, (y + 1) % 4), device(x, core, z, (y + 3) % 4)]
    x_next = [device((x + 1) % 4, core, z, y), device((x + 3) % 4, core, z, y)]
    mate = device(x, 1 - core, z, y)
    me = z * 4 + y
    peers = [(dz, dy) for dz in (2, 1, 3, 0) for dy in (2, 1, 3, 0) if dz or dy]
    greet([device(x, core, (z + dz) % 4, (y + dy) % 4) for dz, dy in peers] + x_next + [mate])
    left, right = pl.ds(0, 384), pl.ds(384, 384)
    a1 = Ring(z, lambda j, h: dq_ref.at[j, pl.ds(2 * h, 2), :, left], z_next, a1_buf, a1_acc, ssem.at[0], rsem.at[0])
    b1 = Ring(y, lambda j, h: dq_ref.at[pl.ds(2 * h, 2), j, :, right], y_next, b1_buf, b1_acc, ssem.at[1], rsem.at[1])
    a2 = Ring(y, lambda j, h: a1_sum.at[j, pl.ds(128 * h, 128)], y_next, a2_buf, a2_acc, ssem.at[2], rsem.at[2])
    b2 = Ring(z, lambda j, h: b1_sum.at[j, pl.ds(128 * h, 128)], z_next, b2_buf, b2_acc, ssem.at[3], rsem.at[3])
    xr = Ring(x, lambda j, h: x_sum.at[j, h], x_next, x_buf, x_acc, ssem.at[4], rsem.at[4])
    cores = []
    for k, step in enumerate((2, 1, 3, 0)):
        place = (x + step) % 4
        cores.append(remote(dp_ref.at[place, 1 - core], core_buf.at[k], core_ssem.at[k], core_rsem.at[k], mate))
    cores[0].start()
    a1.ahead()
    b1.ahead()
    cores[1].start()
    a1.raw()
    b1.raw()
    cores[2].start()
    cores[3].start()

    def add_core(k, step):
        place = (x + step) % 4
        cores[k].wait_recv()
        for h in range(2):
            x_sum[place, h] = (dp_ref[place, core, h].astype(F32) + core_buf[k, h].astype(F32)).astype(BF16)

    add_core(0, 2)
    xr.ahead()
    add_core(1, 1)
    add_core(2, 3)
    xr.raw()
    add_core(3, 0)
    a1.forward()
    b1.forward()
    xr.forward()
    for h in range(2):
        a1_sum[pl.ds(2 * h, 2)] = a1.result(h).astype(BF16)
    a2.ahead()
    a2.raw()
    for h in range(2):
        b1_sum[pl.ds(2 * h, 2)] = b1.result(h).astype(BF16)
    b2.ahead()
    b2.raw()
    a2.forward()
    b2.forward()
    for h in range(2):
        res = xr.result(h).astype(BF16)
        for n in range(16):
            back[n, pl.ds(48 * h, 48), :] = res[:, n * 256 : n * 256 + 256]
    returns = []
    for dz, dy in peers:
        tz, ty = (z + dz) % 4, (y + dy) % 4
        c = remote(back.at[tz * 4 + ty], got.at[me], back_ssem.at[tz * 4 + ty], back_rsem.at[me], device(x, core, tz, ty))
        c.start()
        returns.append(c)
    for h in range(2):
        qg_ref[pl.ds(128 * h, 128), left] = a2.result(h).astype(BF16)
        qg_ref[pl.ds(128 * h, 128), right] = b2.result(h).astype(BF16)
    def lay(n, shard):
        rows = shard.astype(F32).T.astype(BF16)
        for b in range(NB):
            pg_ref[b, n] = rows[b * SL : b * SL + SL, :]

    lay(me, back[me])
    for dz, dy in peers:
        n = (z + dz) % 4 * 4 + (y + dy) % 4
        remote(back.at[n], got.at[n], back_ssem.at[n], back_rsem.at[n], device(x, core, (z + dz) % 4, (y + dy) % 4)).wait_recv()
        lay(n, got[n])
    for ring in (a1, b1, a2, b2, xr):
        ring.drain()
    for c in returns:
        c.wait_send()
    for c in cores:
        c.wait_send()


SMEM = pl.BlockSpec(memory_space=pltpu.SMEM)
VMEM = pl.BlockSpec(memory_space=pltpu.VMEM)
ANY = pl.BlockSpec(memory_space=pl.ANY)


def distribute(passages):
    return pl.pallas_call(
        distribute_kernel,
        out_shape=jax.ShapeDtypeStruct((NB, 16, SL, D), BF16),
        in_specs=[ANY],
        out_specs=ANY,
        scratch_shapes=[pltpu.SemaphoreType.DMA] + [pltpu.SemaphoreType.DMA((16,))] * 2
        + [pltpu.SemaphoreType.DMA((4,))] * 6,
        compiler_params=pltpu.CompilerParams(collective_id=3, has_side_effects=True),
        name="distribute",
    )(passages.reshape(NB, 16, SL, D))


def forward(tiles, rows, queries, sel):
    return pl.pallas_call(
        forward_kernel,
        out_shape=[
            jax.ShapeDtypeStruct((NB, LISTED * SL, BLK), BF16),
            jax.ShapeDtypeStruct((NB, LISTED * SL, D), BF16),
            jax.ShapeDtypeStruct((16, BLK), F32),
        ],
        in_specs=[SMEM, VMEM, ANY, ANY],
        out_specs=[VMEM, VMEM, VMEM],
        scratch_shapes=[
            pltpu.VMEM((NB, BLK, D), BF16),
            pltpu.VMEM((NB, 16, SL, D), BF16),
            pltpu.SemaphoreType.DMA((NB,)),
            pltpu.SemaphoreType.DMA,
        ],
        compiler_params=pltpu.CompilerParams(vmem_limit_bytes=56 * 2**20),
        name="forward",
    )(tiles, rows, queries, sel)


def backward(tiles, rows, m, everyone, e, pq, queries):
    return pl.pallas_call(
        backward_kernel,
        out_shape=[
            jax.ShapeDtypeStruct((NB, BLK, D), BF16),
            jax.ShapeDtypeStruct((D, NB * BLK), BF16),
        ],
        in_specs=[SMEM] + [VMEM] * 6,
        out_specs=[VMEM, VMEM],
        scratch_shapes=[
            pltpu.VMEM((NB, LISTED + 1, SL, D), F32),
            pltpu.SMEM((NB, 64), jnp.int32),
        ],
        compiler_params=pltpu.CompilerParams(vmem_limit_bytes=58 * 2**20),
        name="backward",
    )(tiles, rows, m, everyone, e, pq, queries)


def combine(rows):
    return pl.pallas_call(
        stats_kernel,
        out_shape=[jax.ShapeDtypeStruct((16, BLK), F32), jax.ShapeDtypeStruct((1, 256), F32)],
        in_specs=[VMEM],
        out_specs=[VMEM, VMEM],
        scratch_shapes=[
            pltpu.VMEM((3, 16, BLK), F32),
            pltpu.VMEM((2, 3, 16, BLK), F32),
            pltpu.SemaphoreType.DMA((2, 3)),
            pltpu.SemaphoreType.DMA((2, 3)),
        ],
        compiler_params=pltpu.CompilerParams(collective_id=1, has_side_effects=True),
        name="combine",
    )(rows)


def scatter(dq, dp):
    big, small = (2, 3, 2, 256, 384), (2, 3, 128, 384)
    return pl.pallas_call(
        scatter_kernel,
        out_shape=[jax.ShapeDtypeStruct((256, D), BF16), jax.ShapeDtypeStruct((NB, 16, SL, 96), BF16)],
        in_specs=[VMEM, VMEM],
        out_specs=[VMEM, VMEM],
        scratch_shapes=[
            pltpu.VMEM(big, BF16), pltpu.VMEM((2, 2, 256, 384), BF16), pltpu.VMEM((4, 256, 384), BF16),
            pltpu.VMEM(big, BF16), pltpu.VMEM((2, 2, 256, 384), BF16), pltpu.VMEM((4, 256, 384), BF16),
            pltpu.VMEM(small, BF16), pltpu.VMEM((2, 128, 384), BF16),
            pltpu.VMEM(small, BF16), pltpu.VMEM((2, 128, 384), BF16),
            pltpu.VMEM((2, 3, 48, NB * BLK), BF16), pltpu.VMEM((2, 48, NB * BLK), BF16),
            pltpu.VMEM((4, 2, 48, NB * BLK), BF16),
            pltpu.VMEM((4, 2, 48, NB * BLK), BF16),
            pltpu.VMEM((16, 96, 256), BF16), pltpu.VMEM((16, 96, 256), BF16),
            pltpu.SemaphoreType.DMA((5, 2, 3)), pltpu.SemaphoreType.DMA((5, 2, 3)),
            pltpu.SemaphoreType.DMA((4,)), pltpu.SemaphoreType.DMA((4,)),
            pltpu.SemaphoreType.DMA((16,)), pltpu.SemaphoreType.DMA((16,)),
        ],
        compiler_params=pltpu.CompilerParams(
            collective_id=2, has_side_effects=True, vmem_limit_bytes=56 * 2**20),
        name="scatter",
    )(dq.reshape(4, 4, 256, D), dp.reshape(4, 2, 2, 48, NB * BLK))


def per_device(queries, passages, tiles, positives, cotangent):
    place = (positives % BLK).reshape(NB, BLK).astype(F32)
    rows = jnp.concatenate([cotangent.reshape(NB, BLK), place], axis=0)
    queries = queries.reshape(NB, BLK, D)
    sel = distribute(passages)
    e, pq, stats = forward(tiles, rows, queries, sel)
    everyone, losses = combine(stats)
    dq, dp = backward(tiles, rows, stats, everyone, e, pq, queries)
    query_grads, passage_grads = scatter(dq, dp)
    return losses.reshape(256), query_grads, passage_grads.reshape(NB * BLK, 96)


def solution(mesh):
    in_specs = (P("pb", None), P("pa", None), P(), P("pb"), P("pb"))
    out_specs = (P(("pb", "pa")), P(("pb", "pa"), None), P("pa", "pb"))
    return jax.shard_map(
        per_device, mesh=mesh, in_specs=in_specs, out_specs=out_specs, check_vma=False
    )
```

time: 149 us -> 157 us (1.054)
  Pallas kernels: 137 us -> 148 us
  other arithmetic: 4.45 us -> 1.35 us
    pallas_call x2 -> x3, Pallas kernels: 60.9 us -> 79.3 us  [the longest x1 44.9 us: distribute(): pl.pallas_call(distribute_kernel, out_shape=jax.ShapeDtypeStruct((NB, 16,...]
    pallas_call x1, Pallas kernels: 18.4 us -> 14.2 us  [combine(): pl.pallas_call(stats_kernel, out_shape=[jax.ShapeDtypeStruct((16, BLK), F...]
    pallas_call x1, Pallas kernels: 58.1 us -> 54 us  [scatter(): pl.pallas_call(scatter_kernel, out_shape=[jax.ShapeDtypeStruct((256, D),...]
    convert_element_type x1 -> x0, other arithmetic: 2.38 us -> none  [per_device(): return (losses.reshape(256), query_grads, passage_grads.T.astype(BF16))]
    unnamed x5 -> x6, local copies, waits for them, and re-layouts: 3.69 us -> 5.89 us
where the time goes in v3:
time: 157 us; the launch traced here: 156 us
  Pallas kernels  148 us (94%)
  local copies, waits for them, and re-layouts  6.64 us (4%)
    pallas_call x1, Pallas kernels, scatter(): pl.pallas_call(scatter_kernel, out_shape=[jax.ShapeDtypeStruct((256, D),...  54 us
    pallas_call x1, Pallas kernels, distribute(): pl.pallas_call(distribute_kernel, out_shape=jax.ShapeDtypeStruct((NB, 16,...  44.9 us
    pallas_call x1, Pallas kernels, backward(): pl.pallas_call(backward_kernel, out_shape=[jax.ShapeDtypeStruct((NB, BLK,...  21.4 us
    pallas_call x1, Pallas kernels, combine(): pl.pallas_call(stats_kernel, out_shape=[jax.ShapeDtypeStruct((16, BLK), F...  14.2 us
    pallas_call x1, Pallas kernels, forward(): pl.pallas_call(forward_kernel, out_shape=[jax.ShapeDtypeStruct((NB, LISTE...  13 us
    unnamed x6, local copies, waits for them, and re-layouts  5.89 us

profile of v3, /device:TPU:0, one launch (start us, length us, event | category | flops | bytes accessed | tf_op | source)
XLA Modules:
  0.0 156.2 jit_solution(7825119547596441694)
XLA Ops:
  0.6 1.4 copy.8.tiles_ref
  2.0 0.7 fusion.1
  2.7 0.7 reshape.29
  3.5 0.6 pad_maximum_fusion.rows_ref
  4.1 44.9 %distribute.1.sel_hbm = bf16[4,16,64,768]{3,2,1,0:T(8,128)(2,1)} custom-call(bf16[4,16,64,768]{3,2,1,0:T(8,128)(2,1)} %bitcast.8), custom_call_target="tpu_custom_call" | custom-call | tf_op jit(solution)/shard_map/distribute/pallas_call | solution.py:320
  49.0 13.0 %forward.1 = (bf16[4,512,1024]{2,1,0:T(8,128)(2,1)}, bf16[4,512,768]{2,1,0:T(8,128)(2,1)}, f32[16,1024]{1,0:T(8,128)}) custom-call(s32[32,8]{1,0:T(8,128)} %copy.8.tiles_ref, f32[8,1024]{1,0:T(8,128)} %pad_maximum_fusion.rows_ref, bf16[4,1024,768]{2,1,0:T(8,128)(2,1)} %bitcast.6, bf16[4,16,64,768]{3,2,1,0:T(8,128)(2,1)} %distribute.1.sel_hbm), custom_call_target="tpu_custom_call" | custom-call | tf_op jit(solution)/shard_map/forward/pallas_call | solution.py:333
  62.1 14.2 %combine.1 = (f32[16,1024]{1,0:T(8,128)}, f32[1,256]{1,0:T(1,128)}) custom-call(f32[16,1024]{1,0:T(8,128)} %get-tuple-element.12.rows_ref.m_ref), custom_call_target="tpu_custom_call" | custom-call | tf_op jit(solution)/shard_map/combine/pallas_call | solution.py:372
  76.3 21.4 %backward.1 = (bf16[4,1024,768]{2,1,0:T(8,128)(2,1)}, bf16[768,4096]{1,0:T(8,128)(2,1)}) custom-call(s32[32,8]{1,0:T(8,128)} %copy.8.tiles_ref, f32[8,1024]{1,0:T(8,128)} %pad_maximum_fusion.rows_ref, f32[16,1024]{1,0:T(8,128)} %get-tuple-element.12.rows_ref.m_ref, f32[16,1024]{1,0:T(8,128)} %get-tuple-element.14.all_ref, ...), custom_call_target="tpu_custom_call" | custom-call | tf_op jit(solution)/shard_map/backward/pallas_call | solution.py:354
  97.7 0.0 copy-start
  97.7 54.0 %scatter.1 = (bf16[256,768]{1,0:T(8,128)(2,1)}, bf16[4,16,64,96]{3,2,1,0:T(8,128)(2,1)}) custom-call(bf16[4,4,256,768]{3,2,1,0:T(8,128)(2,1)} %bitcast.9, bf16[4,2,2,48,4096]{4,3,2,1,0:T(8,128)(2,1)} %bitcast.10), custom_call_target="tpu_custom_call" | custom-call | tf_op jit(solution)/shard_map/scatter/pallas_call | solution.py:390
  151.7 2.2 %copy.10 = bf16[4096,96]{0,1:T(8,128)(2,1)} copy(bf16[4096,96]{1,0:T(8,128)(2,1)} %bitcast.11) | data formatting | bytes 1572864
  153.9 0.0 copy-done
  153.9 0.6 copy.13
  154.5 1.8 %copy.14 = bf16[256,768]{1,0:T(8,128)(2,1)} copy(bf16[256,768]{1,0:T(8,128)(2,1)} %get-tuple-element.28) | data formatting | bytes 786432
  (1 shorter events, 0.0 us)
Async XLA Ops:
  97.7 56.2 %copy-start = (f32[1,256]{1,0:T(1,128)S(1)}, f32[1,256]{1,0:T(1,128)}, u32[]{:S(2)}) copy-start(f32[1,256]{1,0:T(1,128)} %get-tuple-element.13) | copy-start | bytes 3076

commit v4 on v0

v4 whole, which is shorter than its diff:
```python
import jax
import jax.numpy as jnp
from jax import lax
from jax.experimental import pallas as pl
from jax.experimental.pallas import tpu as pltpu
from jax.sharding import PartitionSpec as P

D = 768
BLK = 1024
NB = 4
LISTED = 8
SL = 64
PHASES = 4
PR = SL // PHASES
PIECES = 2
SCALE = D ** (-0.5)
LOG2E = 1.4426950408889634
CH = 256
F32 = jnp.float32
BF16 = jnp.bfloat16


def around():
    group, owner = lax.axis_index("pb"), lax.axis_index("pa")
    return group // 2, group % 2, owner // 4, owner % 4


def device(x, core, z, y):
    return (x * 2 + core, z * 4 + y)


def greet(devices):
    barrier = pltpu.get_barrier_semaphore()
    for dev in devices:
        pl.semaphore_signal(barrier, inc=1, device_id=dev, device_id_type=pl.DeviceIdType.MESH)
    pl.semaphore_wait(barrier, len(devices))


def remote(src, dst, send_sem, recv_sem, dev):
    return pltpu.make_async_remote_copy(
        src_ref=src, dst_ref=dst, send_sem=send_sem, recv_sem=recv_sem,
        device_id=dev, device_id_type=pl.DeviceIdType.MESH)


AHEAD, RAW, SUMMED = 0, 1, 2


class Ring:
    def __init__(self, me, chunk, neighbours, buf, acc, send_sem, recv_sem):
        self.me, self.chunk, self.buf, self.acc = me, chunk, buf, acc
        self.send = lambda d, kind, src: remote(
            src, buf.at[d, kind], send_sem.at[d, kind], recv_sem.at[d, kind], neighbours[d])
        self.sent = {}

    def at(self, step, half):
        return self.chunk((self.me + step) % 4, half)

    def go(self, d, kind, src):
        c = self.send(d, kind, src)
        c.start()
        self.sent[d, kind] = c

    def ahead(self):
        self.go(0, AHEAD, self.at(2, 0))
        self.go(1, AHEAD, self.at(2, 1))

    def raw(self):
        self.go(0, RAW, self.at(1, 1))
        self.go(1, RAW, self.at(3, 0))

    def forward(self):
        for d, step in ((0, 1), (1, 3)):
            self.sent[d, AHEAD].wait_recv()
            self.acc[d] = (self.at(step, d)[...].astype(F32) + self.buf[d, AHEAD].astype(F32)).astype(BF16)
            self.go(d, SUMMED, self.acc.at[d])

    def result(self, half):
        a, b = (SUMMED, RAW) if half == 0 else (RAW, SUMMED)
        self.sent[0, a].wait_recv()
        self.sent[1, b].wait_recv()
        return self.at(0, half)[...].astype(F32) + self.buf[0, a].astype(F32) + self.buf[1, b].astype(F32)

    def drain(self):
        for c in self.sent.values():
            c.wait_send()


class Exchange:
    def __init__(self, now, buf, send_sem, recv_sem, peers):
        self.now, self.buf, self.peers = now, buf, peers
        self.sems = send_sem, recv_sem
        self.sent = {}

    def start(self, stage):
        for d in range(3):
            c = remote(self.now.at[stage], self.buf.at[stage, d], self.sems[0].at[stage, d], self.sems[1].at[stage, d],
                       self.peers[stage][d])
            c.start()
            self.sent[stage, d] = c

    def parts(self, stage):
        for d in range(3):
            self.sent[stage, d].wait_recv()
        return [self.now[stage]] + [self.buf[stage, d] for d in range(3)]

    def drain(self):
        for c in self.sent.values():
            c.wait_send()


def whole_kernel(tiles_ref, pos_ref, ct_ref, q_hbm, p_hbm, losses_ref, qg_ref, pg_ref,
                 q_v, sel_v, pq_v, e_v, part_v, dp_v, slot_s,
                 now, now_buf, pick, pick_buf,
                 a1_buf, a1_acc, a1_sum, b1_buf, b1_acc, b1_sum, a2_buf, a2_acc, b2_buf, b2_acc,
                 x_buf, x_acc, core_buf, back, got,
                 q_sem, own_sem, d_ssem, d_rsem, hand_ssem, hand_rsem, ex_ssem, ex_rsem,
                 r_ssem, r_rsem, core_ssem, core_rsem, back_ssem, back_rsem):
    group, owner = lax.axis_index("pb"), lax.axis_index("pa")
    x, core, z, y = around()
    me = z * 4 + y
    peers = [((z + dz) % 4, (y + dy) % 4) for dz in (2, 1, 3, 0) for dy in (2, 1, 3, 0) if dz or dy]
    z_peers = [device(x, core, (z + d) % 4, y) for d in (1, 2, 3)]
    y_peers = [device(x, core, z, (y + d) % 4) for d in (1, 2, 3)]
    x_next = [device((x + 1) % 4, core, z, y), device((x + 3) % 4, core, z, y)]
    mate = device(x, 1 - core, z, y)
    for b in range(NB):
        pltpu.make_async_copy(q_hbm.at[b], q_v.at[b], q_sem.at[b]).start()
    greet([device(x, core, tz, ty) for tz, ty in peers] + x_next + [mate])

    to = (x + 1 + 2 * core) % 4
    source = (x + 3 + 2 * core) % 4
    x_to, x_from = device(to, core, z, y), device(source, core, z, y)
    mine = (x + core) % 4
    theirs = (source + core) % 4

    def rows(n):
        return pl.ds(n * PR, PR)

    own = pltpu.make_async_copy(p_hbm.at[mine, me], sel_v.at[mine, me], own_sem)
    own.start()
    sends = []

    def fetch(n):
        for tz, ty in peers:
            c = remote(p_hbm.at[mine, tz * 4 + ty, rows(n)], sel_v.at[mine, me, rows(n)],
                       d_ssem.at[n, tz * 4 + ty], d_rsem.at[n, me], device(x, core, tz, ty))
            c.start()
            sends.append(c)

    def hand(n, kind, b, dev):
        return remote(sel_v.at[b, :, rows(n)], sel_v.at[b, :, rows(n)], hand_ssem.at[kind, n], hand_rsem.at[kind, n], dev)

    def hand_on(n):
        hand(n, 0, theirs, x_from).wait_recv()
        c = hand(n, 2, theirs, mate)
        c.start()
        sends.append(c)

    fetch(0)
    fetch(1)
    for b in range(NB):
        def find(p, carry, b=b):
            at = jnp.int32(LISTED)
            for t in range(LISTED):
                at = jnp.where(tiles_ref[group * NB + b, t] == p, t, at)
            slot_s[b, p] = at
            return carry

        lax.fori_loop(0, 64, find, 0)
        part_v[b, LISTED] = jnp.zeros((SL, D), F32)
    now[...] = jnp.zeros_like(now)
    pick[...] = jnp.zeros_like(pick)
    own.wait()
    for n in range(PHASES):
        for tz, ty in peers:
            o = tz * 4 + ty
            remote(p_hbm.at[mine, o, rows(n)], sel_v.at[mine, o, rows(n)], d_ssem.at[n, o], d_rsem.at[n, o],
                   device(x, core, tz, ty)).wait_recv()
        for kind, dev in ((0, x_to), (1, mate)):
            c = hand(n, kind, mine, dev)
            c.start()
            sends.append(c)
        if n + 2 < PHASES:
            fetch(n + 2)
        if n >= 1:
            hand_on(n - 1)
    hand_on(PHASES - 1)
    for n in range(PHASES):
        hand(n, 1, (x + 1 - core) % 4, mate).wait_recv()
        hand(n, 2, (x + 2 + core) % 4, mate).wait_recv()
    for b in range(NB):
        pltpu.make_async_copy(q_hbm.at[b], q_v.at[b], q_sem.at[b]).wait()

    def forward(b, carry):
        for t in range(LISTED):
            block = tiles_ref[group * NB + b, t]
            pq_v[b, pl.ds(t * SL, SL), :] = sel_v[block & 3, block >> 2]
        base = (group * NB + b) * 2 * BLK + owner * SL
        for c in range(BLK // CH):
            r = pl.ds(c * CH, CH)
            s = lax.dot_general(pq_v[b], q_v[b, r, :], (((1,), (1,)), ((), ())), preferred_element_type=F32)
            top = jnp.max(s, axis=0, keepdims=True)
            e = jnp.exp2(s * (SCALE * LOG2E) - top * (SCALE * LOG2E))
            e_v[b, :, r] = e.astype(BF16)
            now[0, pl.ds(b, 1), r] = top * SCALE
            now[0, pl.ds(NB + b, 1), r] = jnp.sum(e, axis=0, keepdims=True)
            at = lax.broadcasted_iota(jnp.int32, (SL, CH), 0) == pos_ref[pl.ds(b, 1), r] - base
            pick[0, pl.ds(b, 1), r] = jnp.sum(jnp.where(at, s[0:SL], 0.0), axis=0, keepdims=True) * SCALE
        return carry

    lax.fori_loop(0, NB, forward, 0)

    stats = Exchange(now, now_buf, ex_ssem.at[0], ex_rsem.at[0], [z_peers, y_peers])
    picks = Exchange(pick, pick_buf, ex_ssem.at[1], ex_rsem.at[1], [z_peers, y_peers])
    stats.start(0)
    picks.start(0)
    for stage in range(2):
        parts = stats.parts(stage)
        high = parts[0][0:4]
        for p in parts[1:]:
            high = jnp.maximum(high, p[0:4])
        total = sum(p[4:8] * jnp.exp(p[0:4] - high) for p in parts)
        now[stage + 1, 0:4] = high
        now[stage + 1, 4:8] = total
        if stage == 0:
            stats.start(1)

    def backward(b, carry):
        one = pl.ds(b, 1)
        weight = ct_ref[one, :] * SCALE
        factor = weight * jnp.exp(now[0, one, :] - now[2, one, :]) / now[2, pl.ds(NB + b, 1), :]
        base = (group * NB + b) * 2 * BLK + owner * SL
        at = lax.broadcasted_iota(jnp.int32, (SL, BLK), 0) == pos_ref[one, :] - base
        e_v[b, 0:SL, :] = (e_v[b, 0:SL, :].astype(F32) * factor - jnp.where(at, weight, 0.0)).astype(BF16)
        e_v[b, SL:, :] = (e_v[b, SL:, :].astype(F32) * factor).astype(BF16)
        part_v[b, 0:LISTED] = jnp.dot(e_v[b], q_v[b], preferred_element_type=F32).reshape(LISTED, SL, D)
        return carry

    lax.fori_loop(0, NB, backward, 0)
    picked = sum(picks.parts(0))
    pick[1] = picked
    picks.start(1)

    def dense(piece):
        def one(n, carry):
            blocks = []
            for o in range(2):
                for k in range(2):
                    p = (2 * n + o) * NB + 2 * piece + k
                    blocks.append(sum(part_v[b, slot_s[b, p]] for b in range(NB)))
            flat = jnp.concatenate(blocks, axis=0).astype(BF16).T
            dp_v[piece, :, :, :, :, pl.ds(pl.multiple_of(n * 256, 256), 256)] = flat.reshape(4, 2, 2, 48, 256)
            return carry

        lax.fori_loop(0, 8, one, 0)

    cores = {}

    def to_core(piece):
        for k, step in enumerate((2, 1, 3, 0)):
            c = remote(dp_v.at[piece, (x + step) % 4, 1 - core], core_buf.at[piece, k],
                       core_ssem.at[piece, k], core_rsem.at[piece, k], mate)
            c.start()
            cores[piece, k] = c

    def add_core(piece, k):
        place = (x + (2, 1, 3, 0)[k]) % 4
        cores[piece, k].wait_recv()
        for h in range(2):
            dp_v[piece, place, core, h] = (
                dp_v[piece, place, core, h].astype(F32) + core_buf[piece, k, h].astype(F32)).astype(BF16)

    for piece in range(PIECES):
        dense(piece)
        to_core(piece)

    for c in sends:
        c.wait_send()

    def product(b):
        for c in range(3):
            r = pl.ds(c * 256, 256)
            out = lax.dot_general(e_v[b], pq_v[b, :, r], (((0,), (0,)), ((), ())), preferred_element_type=F32)
            sel_v[b, :, :, r] = out.astype(BF16).reshape(16, SL, 256)

    z_next = [z_peers[0], z_peers[2]]
    y_next = [y_peers[0], y_peers[2]]
    left, right = pl.ds(0, 384), pl.ds(384, 384)
    a1 = Ring(z, lambda j, h: sel_v.at[j, pl.ds(8 * h, 8), :, left], z_next, a1_buf, a1_acc, r_ssem.at[0], r_rsem.at[0])
    b1 = Ring(y, lambda j, h: sel_v.at[pl.ds(2 * h, 2), pl.ds(4 * j, 4), :, right], y_next, b1_buf, b1_acc,
              r_ssem.at[1], r_rsem.at[1])
    a2 = Ring(y, lambda j, h: a1_sum.at[j, pl.ds(2 * h, 2)], y_next, a2_buf, a2_acc, r_ssem.at[2], r_rsem.at[2])
    b2 = Ring(z, lambda j, h: b1_sum.at[j, pl.ds(2 * h, 2)], z_next, b2_buf, b2_acc, r_ssem.at[3], r_rsem.at[3])
    xr = [Ring(x, lambda j, h, n=n: dp_v.at[n, j, core, h], x_next, x_buf.at[n], x_acc.at[n],
               r_ssem.at[4 + n], r_rsem.at[4 + n]) for n in range(PIECES)]
    returns = []

    def go_back(piece):
        for h in range(2):
            res = xr[piece].result(h).astype(BF16)
            for n in range(16):
                back[piece, n, pl.ds(48 * h, 48), :] = res[:, n * 128 : n * 128 + 128]
        for tz, ty in peers:
            o = tz * 4 + ty
            c = remote(back.at[piece, o], got.at[piece, me], back_ssem.at[piece, o], back_rsem.at[piece, me],
                       device(x, core, tz, ty))
            c.start()
            returns.append(c)

    product((z + 2) % 4)
    a1.ahead()
    add_core(0, 0)
    xr[0].ahead()
    add_core(0, 1)
    add_core(0, 2)
    xr[0].raw()
    product((z + 1) % 4)
    product((z + 3) % 4)
    a1.raw()
    add_core(0, 3)
    for k in range(4):
        add_core(1, k)
        if k == 0:
            xr[1].ahead()
        if k == 2:
            xr[1].raw()
    xr[0].forward()
    product(z)
    b1.ahead()
    b1.raw()
    a1.forward()
    xr[1].forward()
    b1.forward()
    go_back(0)
    for h in range(2):
        a1_sum[pl.ds(2 * h, 2)] = a1.result(h).astype(BF16).reshape(2, 4, SL, 384)
    a2.ahead()
    a2.raw()
    for h in range(2):
        b1_sum[pl.ds(2 * h, 2)] = b1.result(h).astype(BF16)
    b2.ahead()
    b2.raw()
    go_back(1)
    a2.forward()
    b2.forward()
    picked = sum(picks.parts(1))
    pick[2] = picked
    span = pl.ds(pl.multiple_of(y * 256, 256), 256)
    losses_ref[...] = now[2, pl.ds(z, 1), span] + jnp.log(now[2, pl.ds(4 + z, 1), span]) - pick[2, pl.ds(z, 1), span]

    def lay(piece, n, shard):
        out = shard.astype(F32).T.astype(BF16)
        for k in range(2):
            pg_ref[2 * piece + k, n] = out[k * SL : k * SL + SL, :]

    for piece in range(PIECES):
        lay(piece, me, back[piece, me])
    for piece in range(PIECES):
        for tz, ty in peers:
            n = tz * 4 + ty
            remote(back.at[piece, n], got.at[piece, n], back_ssem.at[piece, n], back_rsem.at[piece, n],
                   device(x, core, tz, ty)).wait_recv()
            lay(piece, n, got[piece, n])
    for h in range(2):
        qg_ref[pl.ds(128 * h, 128), left] = a2.result(h).astype(BF16).reshape(128, 384)
        qg_ref[pl.ds(128 * h, 128), right] = b2.result(h).astype(BF16).reshape(128, 384)
    for part in [stats, picks, a1, b1, a2, b2] + xr:
        part.drain()
    for c in list(cores.values()) + returns:
        c.wait_send()


SMEM = pl.BlockSpec(memory_space=pltpu.SMEM)
VMEM = pl.BlockSpec(memory_space=pltpu.VMEM)
ANY = pl.BlockSpec(memory_space=pl.ANY)


def whole(tiles, positives, cotangent, queries, passages):
    dma = pltpu.SemaphoreType.DMA
    return pl.pallas_call(
        whole_kernel,
        out_shape=[
            jax.ShapeDtypeStruct((1, 256), F32),
            jax.ShapeDtypeStruct((256, D), BF16),
            jax.ShapeDtypeStruct((NB, 16, SL, 96), BF16),
        ],
        in_specs=[SMEM, VMEM, VMEM, ANY, ANY],
        out_specs=[VMEM, VMEM, VMEM],
        scratch_shapes=[
            pltpu.VMEM((NB, BLK, D), BF16),
            pltpu.VMEM((NB, 16, SL, D), BF16),
            pltpu.VMEM((NB, LISTED * SL, D), BF16),
            pltpu.VMEM((NB, LISTED * SL, BLK), BF16),
            pltpu.VMEM((NB, LISTED + 1, SL, D), F32),
            pltpu.VMEM((PIECES, 4, 2, 2, 48, 2048), BF16),
            pltpu.SMEM((NB, 64), jnp.int32),
            pltpu.VMEM((3, 8, BLK), F32), pltpu.VMEM((2, 3, 8, BLK), F32),
            pltpu.VMEM((3, 8, BLK), F32), pltpu.VMEM((2, 3, 8, BLK), F32),
            pltpu.VMEM((2, 3, 8, SL, 384), BF16), pltpu.VMEM((2, 8, SL, 384), BF16),
            pltpu.VMEM((4, 4, SL, 384), BF16),
            pltpu.VMEM((2, 3, 2, 4, SL, 384), BF16), pltpu.VMEM((2, 2, 4, SL, 384), BF16),
            pltpu.VMEM((4, 4, SL, 384), BF16),
            pltpu.VMEM((2, 3, 2, SL, 384), BF16), pltpu.VMEM((2, 2, SL, 384), BF16),
            pltpu.VMEM((2, 3, 2, SL, 384), BF16), pltpu.VMEM((2, 2, SL, 384), BF16),
            pltpu.VMEM((PIECES, 2, 3, 48, 2048), BF16), pltpu.VMEM((PIECES, 2, 48, 2048), BF16),
            pltpu.VMEM((PIECES, 4, 2, 48, 2048), BF16),
            pltpu.VMEM((PIECES, 16, 96, 128), BF16), pltpu.VMEM((PIECES, 16, 96, 128), BF16),
            dma((NB,)), dma,
            dma((PHASES, 16)), dma((PHASES, 16)),
            dma((3, PHASES)), dma((3, PHASES)),
            dma((2, 2, 3)), dma((2, 2, 3)),
            dma((6, 2, 3)), dma((6, 2, 3)),
            dma((PIECES, 4)), dma((PIECES, 4)),
            dma((PIECES, 16)), dma((PIECES, 16)),
        ],
        compiler_params=pltpu.CompilerParams(
            collective_id=1, has_side_effects=True, vmem_limit_bytes=62 * 2**20),
        name="whole",
    )(tiles, positives, cotangent, queries, passages)


def per_device(queries, passages, tiles, positives, cotangent):
    losses, query_grads, passage_grads = whole(
        tiles, positives.reshape(NB, BLK), cotangent.reshape(NB, BLK),
        queries.reshape(NB, BLK, D), passages.reshape(NB, 16, SL, D))
    return losses.reshape(256), query_grads, passage_grads.reshape(NB * BLK, 96)


def solution(mesh):
    in_specs = (P("pb", None), P("pa", None), P(), P("pb"), P("pb"))
    out_specs = (P(("pb", "pa")), P(("pb", "pa"), None), P("pa", "pb"))
    return jax.shard_map(
        per_device, mesh=mesh, in_specs=in_specs, out_specs=out_specs, check_vma=False
    )
```

time: 610 us -> 125 us (0.20)
  waiting for transfers between devices: 210 us -> 0 us
  blocking collectives: 156 us -> 0 us
  Pallas kernels: 0 us -> 115 us
  matrix products: 88 us -> 0 us
  local copies, waits for them, and re-layouts: 62.4 us -> 9.22 us
  loops' own time: 38.7 us -> 0 us
  other arithmetic: 38.1 us -> 0 us
  between operations: 14.1 us -> 0.64 us
    reduce_scatter x2 -> x0, waiting for transfers between devices: 210 us -> none  [the longest x1 125 us: per_device(): lax.psum_scatter(passage_acc.astype(jnp.bfloat16), 'pb', scatter_dimensio...]
    pallas_call x0 -> x1, Pallas kernels: none -> 115 us  [whole(): pl.pallas_call(whole_kernel, out_shape=[jax.ShapeDtypeStruct((1, 256), F3...]
    dot_general x16 -> x0, matrix products: 88 us -> none  [the longest x8 38.1 us: tile_scores(): lax.dot_general(query_tile, passage_tile, (((1,), (1,)), ((), ())), prefe...]
    pmax x1 -> x0, blocking collectives: 86.3 us -> none  [per_device(): peak = lax.pmax(highs, 'pa')]
    psum x1 -> x0, blocking collectives: 69.6 us -> none  [per_device(): totals, picked = lax.psum((totals * jnp.exp(highs - peak), picked), 'pa')]
    another operation x2 -> x0, loops' own time: 38.7 us -> none  [the longest x1 19.5 us: per_device(): highs, totals, picked = lax.fori_loop(0, count, forward, start)]
    dynamic_slice x42 -> x0, local copies, waits for them, and re-layouts: 28.9 us -> none  [the longest x8 18.3 us: backward(): lax.dynamic_slice_in_dim(passage_acc, col_block * block_rows, block_rows, 0)]
    dynamic_update_slice x8 -> x0, local copies, waits for them, and re-layouts: 16.9 us -> none  [backward(): lax.dynamic_update_slice_in_dim(passage_acc, passage_old + passage_term,...]
  transfers between devices with their start and end apart: 2 -> 0, of which waited for: 2 -> 0; matrix products, arithmetic and copies ran while one was open for 1% -> 0% of each run, Pallas kernels for 0% -> 0%
where the time goes in v4:
time: 125 us
  Pallas kernels  115 us (92%)
  local copies, waits for them, and re-layouts  9.22 us (7%)
    pallas_call x1, Pallas kernels, whole(): pl.pallas_call(whole_kernel, out_shape=[jax.ShapeDtypeStruct((1, 256), F3...  115 us
    unnamed x4, local copies, waits for them, and re-layouts  6.57 us

profile of v4, /device:TPU:0, one launch (start us, length us, event | category | flops | bytes accessed | tf_op | source)
XLA Modules:
  0.0 124.7 jit_solution(5466005122323537005)
XLA Ops:
  0.6 1.4 %copy.8.tiles_ref = s32[32,8]{1,0:T(8,128)} copy(s32[32,8]{0,1:T(8,128)} %param.7) | data formatting | bytes 2048 | tf_op args[2]
  2.0 1.3 %reshape.24.pos_ref = s32[4,1024]{1,0:T(4,128)} reshape(s32[4096]{0:T(1024)} %param.8) | data formatting | bytes 32768 | tf_op jit(solution)/shard_map/reshape | solution.py:424
  3.3 1.3 %reshape.25.ct_ref = f32[4,1024]{1,0:T(4,128)} reshape(f32[4096]{0:T(1024)} %param.9) | data formatting | bytes 32768 | tf_op jit(solution)/shard_map/reshape | solution.py:424
  4.7 114.8 %whole.1 = (f32[1,256]{1,0:T(1,128)}, bf16[256,768]{1,0:T(8,128)(2,1)}, bf16[4,16,64,96]{3,2,1,0:T(8,128)(2,1)}) custom-call(s32[32,8]{1,0:T(8,128)} %copy.8.tiles_ref, s32[4,1024]{1,0:T(4,128)} %reshape.24.pos_ref, f32[4,1024]{1,0:T(4,128)} %reshape.25.ct_ref, bf16[4,1024,768]{2,1,0:T(8,128)(2,1)} %bitcast.4, bf16[4,16,64,768]{3,2,1,0:T(8,128)(2,1)} %bitcast.5), custom_call_target="tpu_custom_call" | custom-call | tf_op jit(solution)/shard_map/whole/pallas_call | solution.py:380
  119.5 2.2 %copy.9 = bf16[4096,96]{0,1:T(8,128)(2,1)} copy(bf16[4096,96]{1,0:T(8,128)(2,1)} %bitcast.6) | data formatting | bytes 1572864
  121.7 1.2 copy.12
  122.9 1.8 %copy.13 = bf16[256,768]{1,0:T(8,128)(2,1)} copy(bf16[256,768]{1,0:T(8,128)(2,1)} %get-tuple-element.16) | data formatting | bytes 786432

commit v5 on v4

--- a/solution.py
+++ b/solution.py
@@ -10,8 +10,8 @@
 NB = 4
 LISTED = 8
 SL = 64
-PHASES = 4
-PR = SL // PHASES
+PHASES = ((0, 16, 0, 384), (0, 16, 384, 384), (16, 16, 0, D), (32, 16, 0, D), (48, 16, 0, 384), (48, 16, 384, 384))
+AT_ONCE = 3
 PIECES = 2
 SCALE = D ** (-0.5)
 LOG2E = 1.4426950408889634
@@ -109,8 +109,7 @@
 
 
 def whole_kernel(tiles_ref, pos_ref, ct_ref, q_hbm, p_hbm, losses_ref, qg_ref, pg_ref,
-                 q_v, sel_v, pq_v, e_v, part_v, dp_v, slot_s,
-                 now, now_buf, pick, pick_buf,
+                 q_v, sel_v, pq_v, e_v, part_v, dp_v, slot_s, pos_v, ct_v, now, now_buf,
                  a1_buf, a1_acc, a1_sum, b1_buf, b1_acc, b1_sum, a2_buf, a2_acc, b2_buf, b2_acc,
                  x_buf, x_acc, core_buf, back, got,
                  q_sem, own_sem, d_ssem, d_rsem, hand_ssem, hand_rsem, ex_ssem, ex_rsem,
@@ -133,8 +132,9 @@
     mine = (x + core) % 4
     theirs = (source + core) % 4
 
-    def rows(n):
-        return pl.ds(n * PR, PR)
+    def part(ref, n):
+        row, rows, col, cols = PHASES[n]
+        return ref.at[..., pl.ds(row, rows), pl.ds(col, cols)]
 
     own = pltpu.make_async_copy(p_hbm.at[mine, me], sel_v.at[mine, me], own_sem)
     own.start()
@@ -142,13 +142,13 @@
 
     def fetch(n):
         for tz, ty in peers:
-            c = remote(p_hbm.at[mine, tz * 4 + ty, rows(n)], sel_v.at[mine, me, rows(n)],
+            c = remote(part(p_hbm.at[mine, tz * 4 + ty], n), part(sel_v.at[mine, me], n),
                        d_ssem.at[n, tz * 4 + ty], d_rsem.at[n, me], device(x, core, tz, ty))
             c.start()
             sends.append(c)
 
     def hand(n, kind, b, dev):
-        return remote(sel_v.at[b, :, rows(n)], sel_v.at[b, :, rows(n)], hand_ssem.at[kind, n], hand_rsem.at[kind, n], dev)
+        return remote(part(sel_v.at[b], n), part(sel_v.at[b], n), hand_ssem.at[kind, n], hand_rsem.at[kind, n], dev)
 
     def hand_on(n):
         hand(n, 0, theirs, x_from).wait_recv()
@@ -156,44 +156,47 @@
         c.start()
         sends.append(c)
 
-    fetch(0)
-    fetch(1)
+    for n in range(AT_ONCE):
+        fetch(n)
     for b in range(NB):
         def find(p, carry, b=b):
             at = jnp.int32(LISTED)
             for t in range(LISTED):
-                at = jnp.where(tiles_ref[group * NB + b, t] == p, t, at)
+                at = jnp.where(tiles_ref[t, group * NB + b] == p, t, at)
             slot_s[b, p] = at
             return carry
 
         lax.fori_loop(0, 64, find, 0)
-        part_v[b, LISTED] = jnp.zeros((SL, D), F32)
+        part_v[b, LISTED] = jnp.zeros((SL, D), BF16)
+        for n in range(8):
+            pos_v[b : b + 1, n * 128 : n * 128 + 128] = pos_ref[8 * b + n : 8 * b + n + 1, :]
+            ct_v[b : b + 1, n * 128 : n * 128 + 128] = ct_ref[8 * b + n : 8 * b + n + 1, :]
     now[...] = jnp.zeros_like(now)
-    pick[...] = jnp.zeros_like(pick)
     own.wait()
-    for n in range(PHASES):
+    for n in range(len(PHASES)):
         for tz, ty in peers:
             o = tz * 4 + ty
-            remote(p_hbm.at[mine, o, rows(n)], sel_v.at[mine, o, rows(n)], d_ssem.at[n, o], d_rsem.at[n, o],
+            remote(part(p_hbm.at[mine, o], n), part(sel_v.at[mine, o], n), d_ssem.at[n, o], d_rsem.at[n, o],
                    device(x, core, tz, ty)).wait_recv()
         for kind, dev in ((0, x_to), (1, mate)):
             c = hand(n, kind, mine, dev)
             c.start()
             sends.append(c)
-        if n + 2 < PHASES:
-            fetch(n + 2)
+        if n + AT_ONCE < len(PHASES):
+            fetch(n + AT_ONCE)
         if n >= 1:
             hand_on(n - 1)
-    hand_on(PHASES - 1)
-    for n in range(PHASES):
+    hand_on(len(PHASES) - 1)
+    for n in range(len(PHASES)):
         hand(n, 1, (x + 1 - core) % 4, mate).wait_recv()
         hand(n, 2, (x + 2 + core) % 4, mate).wait_recv()
     for b in range(NB):
         pltpu.make_async_copy(q_hbm.at[b], q_v.at[b], q_sem.at[b]).wait()
 
-    def forward(b, carry):
+    def forward(half, k):
+        b = 2 * half + k
         for t in range(LISTED):
-            block = tiles_ref[group * NB + b, t]
+            block = tiles_ref[t, group * NB + b]
             pq_v[b, pl.ds(t * SL, SL), :] = sel_v[block & 3, block >> 2]
         base = (group * NB + b) * 2 * BLK + owner * SL
         for c in range(BLK // CH):
@@ -202,57 +205,66 @@
             top = jnp.max(s, axis=0, keepdims=True)
             e = jnp.exp2(s * (SCALE * LOG2E) - top * (SCALE * LOG2E))
             e_v[b, :, r] = e.astype(BF16)
-            now[0, pl.ds(b, 1), r] = top * SCALE
-            now[0, pl.ds(NB + b, 1), r] = jnp.sum(e, axis=0, keepdims=True)
-            at = lax.broadcasted_iota(jnp.int32, (SL, CH), 0) == pos_ref[pl.ds(b, 1), r] - base
-            pick[0, pl.ds(b, 1), r] = jnp.sum(jnp.where(at, s[0:SL], 0.0), axis=0, keepdims=True) * SCALE
-        return carry
-
-    lax.fori_loop(0, NB, forward, 0)
-
-    stats = Exchange(now, now_buf, ex_ssem.at[0], ex_rsem.at[0], [z_peers, y_peers])
-    picks = Exchange(pick, pick_buf, ex_ssem.at[1], ex_rsem.at[1], [z_peers, y_peers])
-    stats.start(0)
-    picks.start(0)
-    for stage in range(2):
-        parts = stats.parts(stage)
-        high = parts[0][0:4]
+            now[half, 0, pl.ds(k, 1), r] = top * SCALE
+            now[half, 0, pl.ds(2 + k, 1), r] = jnp.sum(e, axis=0, keepdims=True)
+            at = lax.broadcasted_iota(jnp.int32, (SL, CH), 0) == pos_v[pl.ds(b, 1), r] - base
+            now[half, 0, pl.ds(4 + k, 1), r] = jnp.sum(jnp.where(at, s[0:SL], 0.0), axis=0, keepdims=True) * SCALE
+
+    def run(body, steps):
+        def one(n, carry):
+            body(n)
+            return carry
+
+        lax.fori_loop(0, steps, one, 0)
+
+    stats = [Exchange(now.at[h], now_buf.at[h], ex_ssem.at[h], ex_rsem.at[h], [z_peers, y_peers]) for h in range(2)]
+
+    def combine(half, stage):
+        parts = stats[half].parts(stage)
+        high = parts[0][0:2]
         for p in parts[1:]:
-            high = jnp.maximum(high, p[0:4])
-        total = sum(p[4:8] * jnp.exp(p[0:4] - high) for p in parts)
-        now[stage + 1, 0:4] = high
-        now[stage + 1, 4:8] = total
+            high = jnp.maximum(high, p[0:2])
+        now[half, stage + 1, 0:2] = high
+        now[half, stage + 1, 2:4] = sum(p[2:4] * jnp.exp(p[0:2] - high) for p in parts)
+        now[half, stage + 1, 4:6] = sum(p[4:6] for p in parts)
         if stage == 0:
-            stats.start(1)
-
-    def backward(b, carry):
-        one = pl.ds(b, 1)
-        weight = ct_ref[one, :] * SCALE
-        factor = weight * jnp.exp(now[0, one, :] - now[2, one, :]) / now[2, pl.ds(NB + b, 1), :]
+            stats[half].start(1)
+
+    run(lambda k: forward(0, k), 2)
+    stats[0].start(0)
+    run(lambda k: forward(1, k), 2)
+    stats[1].start(0)
+    combine(0, 0)
+    combine(1, 0)
+    combine(0, 1)
+
+    def grads(half, k):
+        b = 2 * half + k
+        weight = ct_v[pl.ds(b, 1), :] * SCALE
+        factor = weight * jnp.exp(now[half, 0, pl.ds(k, 1), :] - now[half, 2, pl.ds(k, 1), :]) / now[half, 2, pl.ds(2 + k, 1), :]
         base = (group * NB + b) * 2 * BLK + owner * SL
-        at = lax.broadcasted_iota(jnp.int32, (SL, BLK), 0) == pos_ref[one, :] - base
+        at = lax.broadcasted_iota(jnp.int32, (SL, BLK), 0) == pos_v[pl.ds(b, 1), :] - base
         e_v[b, 0:SL, :] = (e_v[b, 0:SL, :].astype(F32) * factor - jnp.where(at, weight, 0.0)).astype(BF16)
         e_v[b, SL:, :] = (e_v[b, SL:, :].astype(F32) * factor).astype(BF16)
-        part_v[b, 0:LISTED] = jnp.dot(e_v[b], q_v[b], preferred_element_type=F32).reshape(LISTED, SL, D)
-        return carry
-
-    lax.fori_loop(0, NB, backward, 0)
-    picked = sum(picks.parts(0))
-    pick[1] = picked
-    picks.start(1)
-
-    def dense(piece):
-        def one(n, carry):
-            blocks = []
-            for o in range(2):
-                for k in range(2):
-                    p = (2 * n + o) * NB + 2 * piece + k
-                    blocks.append(sum(part_v[b, slot_s[b, p]] for b in range(NB)))
-            flat = jnp.concatenate(blocks, axis=0).astype(BF16).T
-            dp_v[piece, :, :, :, :, pl.ds(pl.multiple_of(n * 256, 256), 256)] = flat.reshape(4, 2, 2, 48, 256)
-            return carry
-
-        lax.fori_loop(0, 8, one, 0)
+
+    def passage_product(b):
+        out = jnp.dot(e_v[b], q_v[b], preferred_element_type=F32)
+        part_v[b, 0:LISTED] = out.astype(BF16).reshape(LISTED, SL, D)
+
+    def query_product(b, quarter):
+        r = pl.ds(pl.multiple_of(quarter * 256, 256), 256)
+        out = lax.dot_general(e_v[b, :, r], pq_v[b], (((0,), (0,)), ((), ())), preferred_element_type=F32)
+        sel_v[b, pl.ds(quarter * 4, 4)] = out.astype(BF16).reshape(4, SL, D)
+
+    def dense(piece, n):
+        blocks = []
+        for o in range(2):
+            for k in range(2):
+                p = (2 * n + o) * NB + 2 * piece + k
+                blocks.append((part_v[0, slot_s[0, p]] + part_v[1, slot_s[1, p]])
+                              + (part_v[2, slot_s[2, p]] + part_v[3, slot_s[3, p]]))
+        flat = jnp.concatenate(blocks, axis=0).T
+        dp_v[piece, :, :, :, :, pl.ds(pl.multiple_of(n * 256, 256), 256)] = flat.reshape(4, 2, 2, 48, 256)
 
     cores = {}
 
@@ -269,19 +281,6 @@
         for h in range(2):
             dp_v[piece, place, core, h] = (
                 dp_v[piece, place, core, h].astype(F32) + core_buf[piece, k, h].astype(F32)).astype(BF16)
-
-    for piece in range(PIECES):
-        dense(piece)
-        to_core(piece)
-
-    for c in sends:
-        c.wait_send()
-
-    def product(b):
-        for c in range(3):
-            r = pl.ds(c * 256, 256)
-            out = lax.dot_general(e_v[b], pq_v[b, :, r], (((0,), (0,)), ((), ())), preferred_element_type=F32)
-            sel_v[b, :, :, r] = out.astype(BF16).reshape(16, SL, 256)
 
     z_next = [z_peers[0], z_peers[2]]
     y_next = [y_peers[0], y_peers[2]]
@@ -307,16 +306,37 @@
             c.start()
             returns.append(c)
 
-    product((z + 2) % 4)
+    def both(k):
+        grads(0, k)
+        passage_product(k)
+
+    run(both, 2)
+    combine(1, 1)
+    run(lambda k: grads(1, k), 2)
+    for c in sends:
+        c.wait_send()
+    run(lambda n: query_product((z + 2) % 4, n), 4)
+    run(lambda n: query_product((z + 3 + n) % 4, (y + 2) % 4), 3)
     a1.ahead()
+    b1.ahead()
+    run(lambda k: passage_product(2 + k), 2)
+
+    def mixed(n):
+        dense(0, n)
+        query_product((z + 1 + 2 * (n // 3)) % 4 * (n < 6) + z * (n >= 6), (y + 3 + n % 3) % 4)
+
+    run(mixed, 8)
+    to_core(0)
+    query_product(z, (y + 1) % 4)
+    a1.raw()
+    b1.raw()
+    run(lambda n: dense(1, n), 8)
+    to_core(1)
     add_core(0, 0)
     xr[0].ahead()
     add_core(0, 1)
     add_core(0, 2)
     xr[0].raw()
-    product((z + 1) % 4)
-    product((z + 3) % 4)
-    a1.raw()
     add_core(0, 3)
     for k in range(4):
         add_core(1, k)
@@ -324,13 +344,10 @@
             xr[1].ahead()
         if k == 2:
             xr[1].raw()
+    a1.forward()
+    b1.forward()
     xr[0].forward()
-    product(z)
-    b1.ahead()
-    b1.raw()
-    a1.forward()
     xr[1].forward()
-    b1.forward()
     go_back(0)
     for h in range(2):
         a1_sum[pl.ds(2 * h, 2)] = a1.result(h).astype(BF16).reshape(2, 4, SL, 384)
@@ -343,29 +360,30 @@
     go_back(1)
     a2.forward()
     b2.forward()
-    picked = sum(picks.parts(1))
-    pick[2] = picked
     span = pl.ds(pl.multiple_of(y * 256, 256), 256)
-    losses_ref[...] = now[2, pl.ds(z, 1), span] + jnp.log(now[2, pl.ds(4 + z, 1), span]) - pick[2, pl.ds(z, 1), span]
-
-    def lay(piece, n, shard):
-        out = shard.astype(F32).T.astype(BF16)
-        for k in range(2):
-            pg_ref[2 * piece + k, n] = out[k * SL : k * SL + SL, :]
+
+    def final(row):
+        return now[z // 2, 2, pl.ds(2 * row + z % 2, 1), span]
+
+    losses_ref[...] = final(0) + jnp.log(final(1)) - final(2)
 
     for piece in range(PIECES):
-        lay(piece, me, back[piece, me])
-    for piece in range(PIECES):
+        got[piece, me] = back[piece, me]
         for tz, ty in peers:
             n = tz * 4 + ty
             remote(back.at[piece, n], got.at[piece, n], back_ssem.at[piece, n], back_rsem.at[piece, n],
                    device(x, core, tz, ty)).wait_recv()
-            lay(piece, n, got[piece, n])
+        for n in range(8):
+            one, two = got[piece, 2 * n], got[piece, 2 * n + 1]
+            for k in range(2):
+                h = slice(k * SL, k * SL + SL)
+                first = (2 * piece + k) * BLK + n * 128
+                pg_ref[:, first : first + 128] = jnp.concatenate([one[:, h], two[:, h]], axis=1)
     for h in range(2):
         qg_ref[pl.ds(128 * h, 128), left] = a2.result(h).astype(BF16).reshape(128, 384)
         qg_ref[pl.ds(128 * h, 128), right] = b2.result(h).astype(BF16).reshape(128, 384)
-    for part in [stats, picks, a1, b1, a2, b2] + xr:
-        part.drain()
+    for moved in stats + [a1, b1, a2, b2] + xr:
+        moved.drain()
     for c in list(cores.values()) + returns:
         c.wait_send()
 
@@ -382,7 +400,7 @@
         out_shape=[
             jax.ShapeDtypeStruct((1, 256), F32),
             jax.ShapeDtypeStruct((256, D), BF16),
-            jax.ShapeDtypeStruct((NB, 16, SL, 96), BF16),
+            jax.ShapeDtypeStruct((96, NB * BLK), BF16),
         ],
         in_specs=[SMEM, VMEM, VMEM, ANY, ANY],
         out_specs=[VMEM, VMEM, VMEM],
@@ -391,11 +409,11 @@
             pltpu.VMEM((NB, 16, SL, D), BF16),
             pltpu.VMEM((NB, LISTED * SL, D), BF16),
             pltpu.VMEM((NB, LISTED * SL, BLK), BF16),
-            pltpu.VMEM((NB, LISTED + 1, SL, D), F32),
+            pltpu.VMEM((NB, LISTED + 1, SL, D), BF16),
             pltpu.VMEM((PIECES, 4, 2, 2, 48, 2048), BF16),
             pltpu.SMEM((NB, 64), jnp.int32),
-            pltpu.VMEM((3, 8, BLK), F32), pltpu.VMEM((2, 3, 8, BLK), F32),
-            pltpu.VMEM((3, 8, BLK), F32), pltpu.VMEM((2, 3, 8, BLK), F32),
+            pltpu.VMEM((8, BLK), jnp.int32), pltpu.VMEM((8, BLK), F32),
+            pltpu.VMEM((2, 3, 8, BLK), F32), pltpu.VMEM((2, 2, 3, 8, BLK), F32),
             pltpu.VMEM((2, 3, 8, SL, 384), BF16), pltpu.VMEM((2, 8, SL, 384), BF16),
             pltpu.VMEM((4, 4, SL, 384), BF16),
             pltpu.VMEM((2, 3, 2, 4, SL, 384), BF16), pltpu.VMEM((2, 2, 4, SL, 384), BF16),
@@ -406,8 +424,8 @@
             pltpu.VMEM((PIECES, 4, 2, 48, 2048), BF16),
             pltpu.VMEM((PIECES, 16, 96, 128), BF16), pltpu.VMEM((PIECES, 16, 96, 128), BF16),
             dma((NB,)), dma,
-            dma((PHASES, 16)), dma((PHASES, 16)),
-            dma((3, PHASES)), dma((3, PHASES)),
+            dma((len(PHASES), 16)), dma((len(PHASES), 16)),
+            dma((3, len(PHASES))), dma((3, len(PHASES))),
             dma((2, 2, 3)), dma((2, 2, 3)),
             dma((6, 2, 3)), dma((6, 2, 3)),
             dma((PIECES, 4)), dma((PIECES, 4)),
@@ -421,9 +439,9 @@
 
 def per_device(queries, passages, tiles, positives, cotangent):
     losses, query_grads, passage_grads = whole(
-        tiles, positives.reshape(NB, BLK), cotangent.reshape(NB, BLK),
+        tiles.T, positives.reshape(32, 128), cotangent.reshape(32, 128),
         queries.reshape(NB, BLK, D), passages.reshape(NB, 16, SL, D))
-    return losses.reshape(256), query_grads, passage_grads.reshape(NB * BLK, 96)
+    return losses.reshape(256), query_grads, passage_grads.T
 
 
 def solution(mesh):

time: 125 us -> 114 us (0.912)
  Pallas kernels: 115 us -> 108 us
  local copies, waits for them, and re-layouts: 9.22 us -> 5.05 us
    pallas_call x1, Pallas kernels: 115 us -> 108 us  [whole(): pl.pallas_call(whole_kernel, out_shape=[jax.ShapeDtypeStruct((1, 256), F3...]
    reshape x2 -> x0, local copies, waits for them, and re-layouts: 2.65 us -> none  [the longest x1 1.33 us: per_device(): positives.reshape(NB, BLK)]
    unnamed x4 -> x3, local copies, waits for them, and re-layouts: 6.57 us -> 5.05 us
where the time goes in v5:
time: 114 us
  Pallas kernels  108 us (95%)
  local copies, waits for them, and re-layouts  5.05 us (4%)
    pallas_call x1, Pallas kernels, whole(): pl.pallas_call(whole_kernel, out_shape=[jax.ShapeDtypeStruct((1, 256), F3...  108 us
    unnamed x3, local copies, waits for them, and re-layouts  5.05 us

profile of v5, /device:TPU:0, one launch (start us, length us, event | category | flops | bytes accessed | tf_op | source)
XLA Modules:
  0.0 113.6 jit_solution(16450716452144837779)
XLA Ops:
  0.6 107.9 %whole.1 = (f32[1,256]{1,0:T(1,128)}, bf16[256,768]{1,0:T(8,128)(2,1)}, bf16[96,4096]{1,0:T(8,128)(2,1)}) custom-call(s32[8,32]{1,0:T(8,128)} %bitcast.12, s32[32,128]{1,0:T(8,128)} %bitcast.10, f32[32,128]{1,0:T(8,128)} %bitcast.11, bf16[4,1024,768]{2,1,0:T(8,128)(2,1)} %bitcast.7, bf16[4,16,64,768]{3,2,1,0:T(8,128)(2,1)} %bitcast.8), custom_call_target="tpu_custom_call" | custom-call | tf_op jit(solution)/shard_map/whole/pallas_call | solution.py:398
  108.6 1.2 %copy.11 = f32[256]{0:T(256)} copy(f32[256]{0:T(256)} %bitcast.13) | data formatting | bytes 2048
  109.8 1.8 %copy.12 = bf16[256,768]{1,0:T(8,128)(2,1)} copy(bf16[256,768]{1,0:T(8,128)(2,1)} %get-tuple-element.13) | data formatting | bytes 786432
  111.5 2.1 %copy.13 = bf16[4096,96]{0,1:T(8,128)(2,1)} copy(bf16[4096,96]{0,1:T(8,128)(2,1)} %bitcast.9) | data formatting | bytes 1572864

commit v6 on v5

--- a/solution.py
+++ b/solution.py
@@ -10,7 +10,7 @@
 NB = 4
 LISTED = 8
 SL = 64
-PHASES = ((0, 16, 0, 384), (0, 16, 384, 384), (16, 16, 0, D), (32, 16, 0, D), (48, 16, 0, 384), (48, 16, 384, 384))
+PHASES = tuple((0, SL, c, 128) for c in range(0, D, 128))
 AT_ONCE = 3
 PIECES = 2
 SCALE = D ** (-0.5)
@@ -108,12 +108,12 @@
             c.wait_send()
 
 
-def whole_kernel(tiles_ref, pos_ref, ct_ref, q_hbm, p_hbm, losses_ref, qg_ref, pg_ref,
-                 q_v, sel_v, pq_v, e_v, part_v, dp_v, slot_s, pos_v, ct_v, now, now_buf,
+def whole_kernel(tiles_ref, pos_ref, ct_ref, q_hbm, p_hbm, losses_ref, qg_ref, got,
+                 q_v, sel_v, pq_v, e_v, part_v, dp_v, slot_s, pos_v, ct_v, now, now_buf, pick, pick_buf,
                  a1_buf, a1_acc, a1_sum, b1_buf, b1_acc, b1_sum, a2_buf, a2_acc, b2_buf, b2_acc,
-                 x_buf, x_acc, core_buf, back, got,
+                 x_buf, x_acc, core_buf, back,
                  q_sem, own_sem, d_ssem, d_rsem, hand_ssem, hand_rsem, ex_ssem, ex_rsem,
-                 r_ssem, r_rsem, core_ssem, core_rsem, back_ssem, back_rsem):
+                 r_ssem, r_rsem, core_ssem, core_rsem, back_ssem, back_rsem, keep_sem):
     group, owner = lax.axis_index("pb"), lax.axis_index("pa")
     x, core, z, y = around()
     me = z * 4 + y
@@ -171,7 +171,6 @@
         for n in range(8):
             pos_v[b : b + 1, n * 128 : n * 128 + 128] = pos_ref[8 * b + n : 8 * b + n + 1, :]
             ct_v[b : b + 1, n * 128 : n * 128 + 128] = ct_ref[8 * b + n : 8 * b + n + 1, :]
-    now[...] = jnp.zeros_like(now)
     own.wait()
     for n in range(len(PHASES)):
         for tz, ty in peers:
@@ -208,7 +207,7 @@
             now[half, 0, pl.ds(k, 1), r] = top * SCALE
             now[half, 0, pl.ds(2 + k, 1), r] = jnp.sum(e, axis=0, keepdims=True)
             at = lax.broadcasted_iota(jnp.int32, (SL, CH), 0) == pos_v[pl.ds(b, 1), r] - base
-            now[half, 0, pl.ds(4 + k, 1), r] = jnp.sum(jnp.where(at, s[0:SL], 0.0), axis=0, keepdims=True) * SCALE
+            pick[0, pl.ds(b, 1), r] = jnp.sum(jnp.where(at, s[0:SL], 0.0), axis=0, keepdims=True) * SCALE
 
     def run(body, steps):
         def one(n, carry):
@@ -217,7 +216,9 @@
 
         lax.fori_loop(0, steps, one, 0)
 
-    stats = [Exchange(now.at[h], now_buf.at[h], ex_ssem.at[h], ex_rsem.at[h], [z_peers, y_peers]) for h in range(2)]
+    turns = [z_peers, y_peers], [y_peers, z_peers]
+    stats = [Exchange(now.at[h], now_buf.at[h], ex_ssem.at[h], ex_rsem.at[h], turns[h]) for h in range(2)]
+    picks = Exchange(pick, pick_buf, ex_ssem.at[2], ex_rsem.at[2], turns[0])
 
     def combine(half, stage):
         parts = stats[half].parts(stage)
@@ -226,7 +227,6 @@
             high = jnp.maximum(high, p[0:2])
         now[half, stage + 1, 0:2] = high
         now[half, stage + 1, 2:4] = sum(p[2:4] * jnp.exp(p[0:2] - high) for p in parts)
-        now[half, stage + 1, 4:6] = sum(p[4:6] for p in parts)
         if stage == 0:
             stats[half].start(1)
 
@@ -292,7 +292,7 @@
     b2 = Ring(z, lambda j, h: b1_sum.at[j, pl.ds(2 * h, 2)], z_next, b2_buf, b2_acc, r_ssem.at[3], r_rsem.at[3])
     xr = [Ring(x, lambda j, h, n=n: dp_v.at[n, j, core, h], x_next, x_buf.at[n], x_acc.at[n],
                r_ssem.at[4 + n], r_rsem.at[4 + n]) for n in range(PIECES)]
-    returns = []
+    returns, keeps = [], []
 
     def go_back(piece):
         for h in range(2):
@@ -305,6 +305,9 @@
                        device(x, core, tz, ty))
             c.start()
             returns.append(c)
+        c = pltpu.make_async_copy(back.at[piece, me], got.at[piece, me], keep_sem.at[piece])
+        c.start()
+        keeps.append(c)
 
     def both(k):
         grads(0, k)
@@ -312,6 +315,7 @@
 
     run(both, 2)
     combine(1, 1)
+    picks.start(0)
     run(lambda k: grads(1, k), 2)
     for c in sends:
         c.wait_send()
@@ -320,72 +324,77 @@
     a1.ahead()
     b1.ahead()
     run(lambda k: passage_product(2 + k), 2)
-
-    def mixed(n):
-        dense(0, n)
-        query_product((z + 1 + 2 * (n // 3)) % 4 * (n < 6) + z * (n >= 6), (y + 3 + n % 3) % 4)
-
-    run(mixed, 8)
+    run(lambda n: dense(0, n), 8)
     to_core(0)
-    query_product(z, (y + 1) % 4)
+    run(lambda n: query_product((z + 1 + 2 * (n // 3)) % 4, (y + 3 + n % 3) % 4), 6)
     a1.raw()
-    b1.raw()
-    run(lambda n: dense(1, n), 8)
-    to_core(1)
     add_core(0, 0)
     xr[0].ahead()
     add_core(0, 1)
     add_core(0, 2)
     xr[0].raw()
+    run(lambda n: query_product(z, (y + 3 + n) % 4), 3)
+    b1.raw()
+    run(lambda n: dense(1, n), 8)
+    to_core(1)
     add_core(0, 3)
-    for k in range(4):
-        add_core(1, k)
-        if k == 0:
-            xr[1].ahead()
-        if k == 2:
-            xr[1].raw()
+    pick[1] = sum(picks.parts(0))
+    picks.start(1)
     a1.forward()
     b1.forward()
+    add_core(1, 0)
+    xr[1].ahead()
     xr[0].forward()
+    add_core(1, 1)
+    add_core(1, 2)
+    xr[1].raw()
+    add_core(1, 3)
     xr[1].forward()
-    go_back(0)
     for h in range(2):
         a1_sum[pl.ds(2 * h, 2)] = a1.result(h).astype(BF16).reshape(2, 4, SL, 384)
     a2.ahead()
     a2.raw()
+    go_back(0)
     for h in range(2):
         b1_sum[pl.ds(2 * h, 2)] = b1.result(h).astype(BF16)
     b2.ahead()
     b2.raw()
-    go_back(1)
     a2.forward()
     b2.forward()
+    go_back(1)
     span = pl.ds(pl.multiple_of(y * 256, 256), 256)
+    pick[2] = sum(picks.parts(1))
 
     def final(row):
         return now[z // 2, 2, pl.ds(2 * row + z % 2, 1), span]
 
-    losses_ref[...] = final(0) + jnp.log(final(1)) - final(2)
-
+    losses_ref[...] = final(0) + jnp.log(final(1)) - pick[2, pl.ds(z, 1), span]
+    for h in range(2):
+        qg_ref[pl.ds(128 * h, 128), left] = a2.result(h).astype(BF16).reshape(128, 384)
+        qg_ref[pl.ds(128 * h, 128), right] = b2.result(h).astype(BF16).reshape(128, 384)
     for piece in range(PIECES):
-        got[piece, me] = back[piece, me]
         for tz, ty in peers:
             n = tz * 4 + ty
             remote(back.at[piece, n], got.at[piece, n], back_ssem.at[piece, n], back_rsem.at[piece, n],
                    device(x, core, tz, ty)).wait_recv()
+    for moved in stats + [picks, a1, b1, a2, b2] + xr:
+        moved.drain()
+    for c in list(cores.values()) + returns:
+        c.wait_send()
+    for c in keeps:
+        c.wait()
+
+
+def lay_kernel(losses_in, qg_in, got, losses_ref, qg_ref, pg_ref):
+    losses_ref[...] = losses_in[...]
+    qg_ref[...] = qg_in[...]
+    for piece in range(PIECES):
         for n in range(8):
             one, two = got[piece, 2 * n], got[piece, 2 * n + 1]
             for k in range(2):
                 h = slice(k * SL, k * SL + SL)
                 first = (2 * piece + k) * BLK + n * 128
                 pg_ref[:, first : first + 128] = jnp.concatenate([one[:, h], two[:, h]], axis=1)
-    for h in range(2):
-        qg_ref[pl.ds(128 * h, 128), left] = a2.result(h).astype(BF16).reshape(128, 384)
-        qg_ref[pl.ds(128 * h, 128), right] = b2.result(h).astype(BF16).reshape(128, 384)
-    for moved in stats + [a1, b1, a2, b2] + xr:
-        moved.drain()
-    for c in list(cores.values()) + returns:
-        c.wait_send()
 
 
 SMEM = pl.BlockSpec(memory_space=pltpu.SMEM)
@@ -400,10 +409,10 @@
         out_shape=[
             jax.ShapeDtypeStruct((1, 256), F32),
             jax.ShapeDtypeStruct((256, D), BF16),
-            jax.ShapeDtypeStruct((96, NB * BLK), BF16),
+            jax.ShapeDtypeStruct((PIECES, 16, 96, 128), BF16),
         ],
         in_specs=[SMEM, VMEM, VMEM, ANY, ANY],
-        out_specs=[VMEM, VMEM, VMEM],
+        out_specs=[VMEM, VMEM, ANY],
         scratch_shapes=[
             pltpu.VMEM((NB, BLK, D), BF16),
             pltpu.VMEM((NB, 16, SL, D), BF16),
@@ -413,7 +422,8 @@
             pltpu.VMEM((PIECES, 4, 2, 2, 48, 2048), BF16),
             pltpu.SMEM((NB, 64), jnp.int32),
             pltpu.VMEM((8, BLK), jnp.int32), pltpu.VMEM((8, BLK), F32),
-            pltpu.VMEM((2, 3, 8, BLK), F32), pltpu.VMEM((2, 2, 3, 8, BLK), F32),
+            pltpu.VMEM((2, 3, 4, BLK), F32), pltpu.VMEM((2, 2, 3, 4, BLK), F32),
+            pltpu.VMEM((3, 4, BLK), F32), pltpu.VMEM((2, 3, 4, BLK), F32),
             pltpu.VMEM((2, 3, 8, SL, 384), BF16), pltpu.VMEM((2, 8, SL, 384), BF16),
             pltpu.VMEM((4, 4, SL, 384), BF16),
             pltpu.VMEM((2, 3, 2, 4, SL, 384), BF16), pltpu.VMEM((2, 2, 4, SL, 384), BF16),
@@ -422,14 +432,14 @@
             pltpu.VMEM((2, 3, 2, SL, 384), BF16), pltpu.VMEM((2, 2, SL, 384), BF16),
             pltpu.VMEM((PIECES, 2, 3, 48, 2048), BF16), pltpu.VMEM((PIECES, 2, 48, 2048), BF16),
             pltpu.VMEM((PIECES, 4, 2, 48, 2048), BF16),
-            pltpu.VMEM((PIECES, 16, 96, 128), BF16), pltpu.VMEM((PIECES, 16, 96, 128), BF16),
+            pltpu.VMEM((PIECES, 16, 96, 128), BF16),
             dma((NB,)), dma,
             dma((len(PHASES), 16)), dma((len(PHASES), 16)),
             dma((3, len(PHASES))), dma((3, len(PHASES))),
-            dma((2, 2, 3)), dma((2, 2, 3)),
+            dma((3, 2, 3)), dma((3, 2, 3)),
             dma((6, 2, 3)), dma((6, 2, 3)),
             dma((PIECES, 4)), dma((PIECES, 4)),
-            dma((PIECES, 16)), dma((PIECES, 16)),
+            dma((PIECES, 16)), dma((PIECES, 16)), dma((PIECES,)),
         ],
         compiler_params=pltpu.CompilerParams(
             collective_id=1, has_side_effects=True, vmem_limit_bytes=62 * 2**20),
@@ -437,10 +447,24 @@
     )(tiles, positives, cotangent, queries, passages)
 
 
+def lay(losses, query_grads, got):
+    return pl.pallas_call(
+        lay_kernel,
+        out_shape=[
+            jax.ShapeDtypeStruct((1, 256), F32),
+            jax.ShapeDtypeStruct((256, D), BF16),
+            jax.ShapeDtypeStruct((96, NB * BLK), BF16),
+        ],
+        in_specs=[VMEM, VMEM, VMEM],
+        out_specs=[VMEM, VMEM, VMEM],
+        name="lay",
+    )(losses, query_grads, got)
+
+
 def per_device(queries, passages, tiles, positives, cotangent):
-    losses, query_grads, passage_grads = whole(
+    losses, query_grads, passage_grads = lay(*whole(
         tiles.T, positives.reshape(32, 128), cotangent.reshape(32, 128),
-        queries.reshape(NB, BLK, D), passages.reshape(NB, 16, SL, D))
+        queries.reshape(NB, BLK, D), passages.reshape(NB, 16, SL, D)))
     return losses.reshape(256), query_grads, passage_grads.T
 
 

time: 114 us -> 106 us (0.930)
  local copies, waits for them, and re-layouts: 5.05 us -> 0 us
  Pallas kernels: 108 us -> 105 us
    pallas_call x1, Pallas kernels: 108 us -> 103 us  [whole(): pl.pallas_call(whole_kernel, out_shape=[jax.ShapeDtypeStruct((1, 256), F3...]
    unnamed x3 -> x0, local copies, waits for them, and re-layouts: 5.05 us -> none
    pallas_call x0 -> x1, Pallas kernels: none -> 2.53 us  [lay(): pl.pallas_call(lay_kernel, out_shape=[jax.ShapeDtypeStruct((1, 256), F32)...]
where the time goes in v6:
time: 106 us
  Pallas kernels  105 us (99%)
    pallas_call x1, Pallas kernels, whole(): pl.pallas_call(whole_kernel, out_shape=[jax.ShapeDtypeStruct((1, 256), F3...  103 us
    pallas_call x1, Pallas kernels, lay(): pl.pallas_call(lay_kernel, out_shape=[jax.ShapeDtypeStruct((1, 256), F32)...  2.53 us

profile of v6, /device:TPU:0, one launch (start us, length us, event | category | flops | bytes accessed | tf_op | source)
XLA Modules:
  0.0 105.7 jit_solution(2816334461620716903)
XLA Ops:
  0.6 102.5 %whole.1 = (f32[1,256]{1,0:T(1,128)}, bf16[256,768]{1,0:T(8,128)(2,1)}, bf16[2,16,96,128]{3,2,1,0:T(8,128)(2,1)}) custom-call(s32[8,32]{1,0:T(8,128)} %bitcast.11, s32[32,128]{1,0:T(8,128)} %bitcast.9, f32[32,128]{1,0:T(8,128)} %bitcast.10, bf16[4,1024,768]{2,1,0:T(8,128)(2,1)} %bitcast.7, bf16[4,16,64,768]{3,2,1,0:T(8,128)(2,1)} %bitcast.8), custom_call_target="tpu_custom_call" | custom-call | tf_op jit(solution)/shard_map/whole/pallas_call | solution.py:407
  103.2 2.5 %lay.1 = (f32[1,256]{1,0:T(1,128)}, bf16[256,768]{1,0:T(8,128)(2,1)}, bf16[96,4096]{1,0:T(8,128)(2,1)}) custom-call(f32[1,256]{1,0:T(1,128)} %get-tuple-element.9.losses_in, bf16[256,768]{1,0:T(8,128)(2,1)} %get-tuple-element.10.qg_in, bf16[2,16,96,128]{3,2,1,0:T(8,128)(2,1)} %get-tuple-element.11.got), custom_call_target="tpu_custom_call" | custom-call | tf_op jit(solution)/shard_map/lay/pallas_call | solution.py:451

commit v7 on v6

--- a/solution.py
+++ b/solution.py
@@ -10,7 +10,7 @@
 NB = 4
 LISTED = 8
 SL = 64
-PHASES = tuple((0, SL, c, 128) for c in range(0, D, 128))
+PHASES = tuple((c, False, True) for c in range(0, 640, 128)) + ((640, False, False), (640, True, False))
 AT_ONCE = 3
 PIECES = 2
 SCALE = D ** (-0.5)
@@ -112,7 +112,7 @@
                  q_v, sel_v, pq_v, e_v, part_v, dp_v, slot_s, pos_v, ct_v, now, now_buf, pick, pick_buf,
                  a1_buf, a1_acc, a1_sum, b1_buf, b1_acc, b1_sum, a2_buf, a2_acc, b2_buf, b2_acc,
                  x_buf, x_acc, core_buf, back,
-                 q_sem, own_sem, d_ssem, d_rsem, hand_ssem, hand_rsem, ex_ssem, ex_rsem,
+                 q_sem, own_sem, d_ssem, d_rsem, hand_ssem, hand_rsem, ex_ssem, ex_rsem, tell_ssem, tell_rsem,
                  r_ssem, r_rsem, core_ssem, core_rsem, back_ssem, back_rsem, keep_sem):
     group, owner = lax.axis_index("pb"), lax.axis_index("pa")
     x, core, z, y = around()
@@ -133,16 +133,20 @@
     theirs = (source + core) % 4
 
     def part(ref, n):
-        row, rows, col, cols = PHASES[n]
-        return ref.at[..., pl.ds(row, rows), pl.ds(col, cols)]
-
-    own = pltpu.make_async_copy(p_hbm.at[mine, me], sel_v.at[mine, me], own_sem)
-    own.start()
+        return ref.at[..., pl.ds(PHASES[n][0], 128)]
+
+    def which(n):
+        return theirs if PHASES[n][1] else mine
+
+    owns = [pltpu.make_async_copy(p_hbm.at[mine, me], sel_v.at[mine, me], own_sem.at[0]),
+            pltpu.make_async_copy(part(p_hbm.at[theirs, me], -1), part(sel_v.at[theirs, me], -1), own_sem.at[1])]
+    for c in owns:
+        c.start()
     sends = []
 
     def fetch(n):
         for tz, ty in peers:
-            c = remote(part(p_hbm.at[mine, tz * 4 + ty], n), part(sel_v.at[mine, me], n),
+            c = remote(part(p_hbm.at[which(n), tz * 4 + ty], n), part(sel_v.at[which(n), me], n),
                        d_ssem.at[n, tz * 4 + ty], d_rsem.at[n, me], device(x, core, tz, ty))
             c.start()
             sends.append(c)
@@ -171,24 +175,25 @@
         for n in range(8):
             pos_v[b : b + 1, n * 128 : n * 128 + 128] = pos_ref[8 * b + n : 8 * b + n + 1, :]
             ct_v[b : b + 1, n * 128 : n * 128 + 128] = ct_ref[8 * b + n : 8 * b + n + 1, :]
-    own.wait()
+    for c in owns:
+        c.wait()
     for n in range(len(PHASES)):
         for tz, ty in peers:
             o = tz * 4 + ty
-            remote(part(p_hbm.at[mine, o], n), part(sel_v.at[mine, o], n), d_ssem.at[n, o], d_rsem.at[n, o],
+            remote(part(p_hbm.at[which(n), o], n), part(sel_v.at[which(n), o], n), d_ssem.at[n, o], d_rsem.at[n, o],
                    device(x, core, tz, ty)).wait_recv()
-        for kind, dev in ((0, x_to), (1, mate)):
-            c = hand(n, kind, mine, dev)
+        for kind, dev in ((0, x_to), (1, mate)) if PHASES[n][2] else ((1, mate),):
+            c = hand(n, kind, which(n), dev)
             c.start()
             sends.append(c)
         if n + AT_ONCE < len(PHASES):
             fetch(n + AT_ONCE)
-        if n >= 1:
+        if n >= 1 and PHASES[n - 1][2]:
             hand_on(n - 1)
-    hand_on(len(PHASES) - 1)
     for n in range(len(PHASES)):
-        hand(n, 1, (x + 1 - core) % 4, mate).wait_recv()
-        hand(n, 2, (x + 2 + core) % 4, mate).wait_recv()
+        hand(n, 1, (x + 2 + core) % 4 if PHASES[n][1] else (x + 1 - core) % 4, mate).wait_recv()
+        if PHASES[n][2]:
+            hand(n, 2, (x + 2 + core) % 4, mate).wait_recv()
     for b in range(NB):
         pltpu.make_async_copy(q_hbm.at[b], q_v.at[b], q_sem.at[b]).wait()
 
@@ -216,32 +221,40 @@
 
         lax.fori_loop(0, steps, one, 0)
 
-    turns = [z_peers, y_peers], [y_peers, z_peers]
-    stats = [Exchange(now.at[h], now_buf.at[h], ex_ssem.at[h], ex_rsem.at[h], turns[h]) for h in range(2)]
-    picks = Exchange(pick, pick_buf, ex_ssem.at[2], ex_rsem.at[2], turns[0])
-
-    def combine(half, stage):
-        parts = stats[half].parts(stage)
+    spread = []
+
+    def tell(half):
+        for tz, ty in peers:
+            c = remote(now.at[half, 0], now_buf.at[half, me], tell_ssem.at[half, tz * 4 + ty], tell_rsem.at[half, me],
+                       device(x, core, tz, ty))
+            c.start()
+            spread.append(c)
+
+    picks = Exchange(pick, pick_buf, ex_ssem, ex_rsem, [z_peers, y_peers])
+
+    def combine(half):
+        parts = [now[half, 0]]
+        for tz, ty in peers:
+            o = tz * 4 + ty
+            remote(now.at[half, 0], now_buf.at[half, o], tell_ssem.at[half, o], tell_rsem.at[half, o],
+                   device(x, core, tz, ty)).wait_recv()
+            parts.append(now_buf[half, o])
         high = parts[0][0:2]
         for p in parts[1:]:
             high = jnp.maximum(high, p[0:2])
-        now[half, stage + 1, 0:2] = high
-        now[half, stage + 1, 2:4] = sum(p[2:4] * jnp.exp(p[0:2] - high) for p in parts)
-        if stage == 0:
-            stats[half].start(1)
+        now[half, 1, 0:2] = high
+        now[half, 1, 2:4] = sum(p[2:4] * jnp.exp(p[0:2] - high) for p in parts)
 
     run(lambda k: forward(0, k), 2)
-    stats[0].start(0)
+    tell(0)
     run(lambda k: forward(1, k), 2)
-    stats[1].start(0)
-    combine(0, 0)
-    combine(1, 0)
-    combine(0, 1)
+    tell(1)
+    combine(0)
 
     def grads(half, k):
         b = 2 * half + k
         weight = ct_v[pl.ds(b, 1), :] * SCALE
-        factor = weight * jnp.exp(now[half, 0, pl.ds(k, 1), :] - now[half, 2, pl.ds(k, 1), :]) / now[half, 2, pl.ds(2 + k, 1), :]
+        factor = weight * jnp.exp(now[half, 0, pl.ds(k, 1), :] - now[half, 1, pl.ds(k, 1), :]) / now[half, 1, pl.ds(2 + k, 1), :]
         base = (group * NB + b) * 2 * BLK + owner * SL
         at = lax.broadcasted_iota(jnp.int32, (SL, BLK), 0) == pos_v[pl.ds(b, 1), :] - base
         e_v[b, 0:SL, :] = (e_v[b, 0:SL, :].astype(F32) * factor - jnp.where(at, weight, 0.0)).astype(BF16)
@@ -314,14 +327,17 @@
         passage_product(k)
 
     run(both, 2)
-    combine(1, 1)
-    picks.start(0)
+    combine(1)
     run(lambda k: grads(1, k), 2)
     for c in sends:
         c.wait_send()
-    run(lambda n: query_product((z + 2) % 4, n), 4)
+    opposite = (z + 2) % 4
+    for c in range(3):
+        r = pl.ds(c * 256, 256)
+        out = lax.dot_general(e_v[opposite], pq_v[opposite, :, r], (((0,), (0,)), ((), ())), preferred_element_type=F32)
+        sel_v[opposite, :, :, r] = out.astype(BF16).reshape(16, SL, 256)
+    a1.ahead()
     run(lambda n: query_product((z + 3 + n) % 4, (y + 2) % 4), 3)
-    a1.ahead()
     b1.ahead()
     run(lambda k: passage_product(2 + k), 2)
     run(lambda n: dense(0, n), 8)
@@ -338,23 +354,24 @@
     run(lambda n: dense(1, n), 8)
     to_core(1)
     add_core(0, 3)
-    pick[1] = sum(picks.parts(0))
-    picks.start(1)
     a1.forward()
     b1.forward()
+    xr[0].forward()
     add_core(1, 0)
     xr[1].ahead()
-    xr[0].forward()
     add_core(1, 1)
     add_core(1, 2)
     xr[1].raw()
     add_core(1, 3)
+    picks.start(0)
+    go_back(0)
+    pick[1] = sum(picks.parts(0))
+    picks.start(1)
     xr[1].forward()
     for h in range(2):
         a1_sum[pl.ds(2 * h, 2)] = a1.result(h).astype(BF16).reshape(2, 4, SL, 384)
     a2.ahead()
     a2.raw()
-    go_back(0)
     for h in range(2):
         b1_sum[pl.ds(2 * h, 2)] = b1.result(h).astype(BF16)
     b2.ahead()
@@ -366,7 +383,7 @@
     pick[2] = sum(picks.parts(1))
 
     def final(row):
-        return now[z // 2, 2, pl.ds(2 * row + z % 2, 1), span]
+        return now[z // 2, 1, pl.ds(2 * row + z % 2, 1), span]
 
     losses_ref[...] = final(0) + jnp.log(final(1)) - pick[2, pl.ds(z, 1), span]
     for h in range(2):
@@ -377,9 +394,9 @@
             n = tz * 4 + ty
             remote(back.at[piece, n], got.at[piece, n], back_ssem.at[piece, n], back_rsem.at[piece, n],
                    device(x, core, tz, ty)).wait_recv()
-    for moved in stats + [picks, a1, b1, a2, b2] + xr:
+    for moved in [picks, a1, b1, a2, b2] + xr:
         moved.drain()
-    for c in list(cores.values()) + returns:
+    for c in list(cores.values()) + returns + spread:
         c.wait_send()
     for c in keeps:
         c.wait()
@@ -422,7 +439,7 @@
             pltpu.VMEM((PIECES, 4, 2, 2, 48, 2048), BF16),
             pltpu.SMEM((NB, 64), jnp.int32),
             pltpu.VMEM((8, BLK), jnp.int32), pltpu.VMEM((8, BLK), F32),
-            pltpu.VMEM((2, 3, 4, BLK), F32), pltpu.VMEM((2, 2, 3, 4, BLK), F32),
+            pltpu.VMEM((2, 2, 4, BLK), F32), pltpu.VMEM((2, 16, 4, BLK), F32),
             pltpu.VMEM((3, 4, BLK), F32), pltpu.VMEM((2, 3, 4, BLK), F32),
             pltpu.VMEM((2, 3, 8, SL, 384), BF16), pltpu.VMEM((2, 8, SL, 384), BF16),
             pltpu.VMEM((4, 4, SL, 384), BF16),
@@ -433,10 +450,10 @@
             pltpu.VMEM((PIECES, 2, 3, 48, 2048), BF16), pltpu.VMEM((PIECES, 2, 48, 2048), BF16),
             pltpu.VMEM((PIECES, 4, 2, 48, 2048), BF16),
             pltpu.VMEM((PIECES, 16, 96, 128), BF16),
-            dma((NB,)), dma,
+            dma((NB,)), dma((2,)),
             dma((len(PHASES), 16)), dma((len(PHASES), 16)),
             dma((3, len(PHASES))), dma((3, len(PHASES))),
-            dma((3, 2, 3)), dma((3, 2, 3)),
+            dma((2, 3)), dma((2, 3)), dma((2, 16)), dma((2, 16)),
             dma((6, 2, 3)), dma((6, 2, 3)),
             dma((PIECES, 4)), dma((PIECES, 4)),
             dma((PIECES, 16)), dma((PIECES, 16)), dma((PIECES,)),

time: 106 us -> 102 us (0.962); the launches traced: 106 us -> 100 us
  Pallas kernels: 105 us -> 99.7 us
    pallas_call x1, Pallas kernels: 103 us -> 97.2 us  [whole(): pl.pallas_call(whole_kernel, out_shape=[jax.ShapeDtypeStruct((1, 256), F3...]
where the time goes in v7:
time: 102 us; the launch traced here: 100 us
  Pallas kernels  99.7 us (98%)
    pallas_call x1, Pallas kernels, whole(): pl.pallas_call(whole_kernel, out_shape=[jax.ShapeDtypeStruct((1, 256), F3...  97.2 us
    pallas_call x1, Pallas kernels, lay(): pl.pallas_call(lay_kernel, out_shape=[jax.ShapeDtypeStruct((1, 256), F32)...  2.53 us

profile of v7, /device:TPU:0, one launch (start us, length us, event | category | flops | bytes accessed | tf_op | source)
XLA Modules:
  0.0 100.4 jit_solution(15892396059595511248)
XLA Ops:
  0.6 97.2 %whole.1 = (f32[1,256]{1,0:T(1,128)}, bf16[256,768]{1,0:T(8,128)(2,1)}, bf16[2,16,96,128]{3,2,1,0:T(8,128)(2,1)}) custom-call(s32[8,32]{1,0:T(8,128)} %bitcast.11, s32[32,128]{1,0:T(8,128)} %bitcast.9, f32[32,128]{1,0:T(8,128)} %bitcast.10, bf16[4,1024,768]{2,1,0:T(8,128)(2,1)} %bitcast.7, bf16[4,16,64,768]{3,2,1,0:T(8,128)(2,1)} %bitcast.8), custom_call_target="tpu_custom_call" | custom-call | tf_op jit(solution)/shard_map/whole/pallas_call | solution.py:424
  97.9 2.5 %lay.1 = (f32[1,256]{1,0:T(1,128)}, bf16[256,768]{1,0:T(8,128)(2,1)}, bf16[96,4096]{1,0:T(8,128)(2,1)}) custom-call(f32[1,256]{1,0:T(1,128)} %get-tuple-element.9.losses_in, bf16[256,768]{1,0:T(8,128)(2,1)} %get-tuple-element.10.qg_in, bf16[2,16,96,128]{3,2,1,0:T(8,128)(2,1)} %get-tuple-element.11.got), custom_call_target="tpu_custom_call" | custom-call | tf_op jit(solution)/shard_map/lay/pallas_call | solution.py:468

commit v8 on v7

--- a/solution.py
+++ b/solution.py
@@ -10,7 +10,10 @@
 NB = 4
 LISTED = 8
 SL = 64
-PHASES = tuple((c, False, True) for c in range(0, 640, 128)) + ((640, False, False), (640, True, False))
+HALF = SL // 2
+PHASES = ((0, 0, False, True), (0, 256, False, True), (0, 512, False, True),
+          (1, 0, False, True), (1, 256, False, True), (1, 512, False, False), (1, 512, True, False))
+EARLY = 3
 AT_ONCE = 3
 PIECES = 2
 SCALE = D ** (-0.5)
@@ -108,8 +111,8 @@
             c.wait_send()
 
 
-def whole_kernel(tiles_ref, pos_ref, ct_ref, q_hbm, p_hbm, losses_ref, qg_ref, got,
-                 q_v, sel_v, pq_v, e_v, part_v, dp_v, slot_s, pos_v, ct_v, now, now_buf, pick, pick_buf,
+def whole_kernel(tiles_ref, pos_hbm, ct_hbm, q_hbm, p_hbm, losses_hbm, qg_hbm, got,
+                 pos_ref, ct_ref, losses_ref, qg_ref, q_v, sel_a, sel_b, dq_v, pq_v, e_v, part_v, dp_v, slot_s, pos_v, ct_v, local, now, now_buf, pick, pick_buf,
                  a1_buf, a1_acc, a1_sum, b1_buf, b1_acc, b1_sum, a2_buf, a2_acc, b2_buf, b2_acc,
                  x_buf, x_acc, core_buf, back,
                  q_sem, own_sem, d_ssem, d_rsem, hand_ssem, hand_rsem, ex_ssem, ex_rsem, tell_ssem, tell_rsem,
@@ -117,6 +120,7 @@
     group, owner = lax.axis_index("pb"), lax.axis_index("pa")
     x, core, z, y = around()
     me = z * 4 + y
+    sel_v = sel_a, sel_b
     peers = [((z + dz) % 4, (y + dy) % 4) for dz in (2, 1, 3, 0) for dy in (2, 1, 3, 0) if dz or dy]
     z_peers = [device(x, core, (z + d) % 4, y) for d in (1, 2, 3)]
     y_peers = [device(x, core, z, (y + d) % 4) for d in (1, 2, 3)]
@@ -124,6 +128,9 @@
     mate = device(x, 1 - core, z, y)
     for b in range(NB):
         pltpu.make_async_copy(q_hbm.at[b], q_v.at[b], q_sem.at[b]).start()
+    small = [pltpu.make_async_copy(pos_hbm, pos_ref, own_sem.at[3]), pltpu.make_async_copy(ct_hbm, ct_ref, own_sem.at[4])]
+    for c in small:
+        c.start()
     greet([device(x, core, tz, ty) for tz, ty in peers] + x_next + [mate])
 
     to = (x + 1 + 2 * core) % 4
@@ -132,27 +139,34 @@
     mine = (x + core) % 4
     theirs = (source + core) % 4
 
-    def part(ref, n):
-        return ref.at[..., pl.ds(PHASES[n][0], 128)]
+    def given(b, s, n):
+        return p_hbm.at[b, s, pl.ds(HALF * PHASES[n][0], HALF), pl.ds(PHASES[n][1], 256)]
+
+    def kept(b, n):
+        return sel_v[PHASES[n][0]].at[b, :, :, pl.ds(PHASES[n][1], 256)]
+
+    def kept_of(b, o, n):
+        return sel_v[PHASES[n][0]].at[b, o, :, pl.ds(PHASES[n][1], 256)]
 
     def which(n):
-        return theirs if PHASES[n][1] else mine
-
-    owns = [pltpu.make_async_copy(p_hbm.at[mine, me], sel_v.at[mine, me], own_sem.at[0]),
-            pltpu.make_async_copy(part(p_hbm.at[theirs, me], -1), part(sel_v.at[theirs, me], -1), own_sem.at[1])]
+        return theirs if PHASES[n][2] else mine
+
+    owns = [pltpu.make_async_copy(p_hbm.at[mine, me, pl.ds(HALF * k, HALF)], sel_v[k].at[mine, me], own_sem.at[k])
+            for k in range(2)]
+    owns.append(pltpu.make_async_copy(given(theirs, me, -1), kept_of(theirs, me, -1), own_sem.at[2]))
     for c in owns:
         c.start()
     sends = []
 
     def fetch(n):
         for tz, ty in peers:
-            c = remote(part(p_hbm.at[which(n), tz * 4 + ty], n), part(sel_v.at[which(n), me], n),
+            c = remote(given(which(n), tz * 4 + ty, n), kept_of(which(n), me, n),
                        d_ssem.at[n, tz * 4 + ty], d_rsem.at[n, me], device(x, core, tz, ty))
             c.start()
             sends.append(c)
 
     def hand(n, kind, b, dev):
-        return remote(part(sel_v.at[b], n), part(sel_v.at[b], n), hand_ssem.at[kind, n], hand_rsem.at[kind, n], dev)
+        return remote(kept(b, n), kept(b, n), hand_ssem.at[kind, n], hand_rsem.at[kind, n], dev)
 
     def hand_on(n):
         hand(n, 0, theirs, x_from).wait_recv()
@@ -162,6 +176,8 @@
 
     for n in range(AT_ONCE):
         fetch(n)
+    for c in small:
+        c.wait()
     for b in range(NB):
         def find(p, carry, b=b):
             at = jnp.int32(LISTED)
@@ -171,59 +187,73 @@
             return carry
 
         lax.fori_loop(0, 64, find, 0)
-        part_v[b, LISTED] = jnp.zeros((SL, D), BF16)
+        part_v[b, :, LISTED] = jnp.zeros((2, HALF, D), BF16)
         for n in range(8):
             pos_v[b : b + 1, n * 128 : n * 128 + 128] = pos_ref[8 * b + n : 8 * b + n + 1, :]
             ct_v[b : b + 1, n * 128 : n * 128 + 128] = ct_ref[8 * b + n : 8 * b + n + 1, :]
     for c in owns:
         c.wait()
+    def forward(half, b):
+        first = half * LISTED * HALF
+        for t in range(LISTED):
+            block = tiles_ref[t, group * NB + b]
+            pq_v[b, pl.ds(first + t * HALF, HALF), :] = sel_v[half][block & 3, block >> 2]
+        base = (group * NB + b) * 2 * BLK + owner * SL + half * HALF
+        for c in range(BLK // CH):
+            r = pl.ds(c * CH, CH)
+            s = lax.dot_general(pq_v[b, pl.ds(first, LISTED * HALF), :], q_v[b, r, :], (((1,), (1,)), ((), ())),
+                                preferred_element_type=F32)
+            top = jnp.max(s, axis=0, keepdims=True)
+            e = jnp.exp2(s * (SCALE * LOG2E) - top * (SCALE * LOG2E))
+            e_v[b, pl.ds(first, LISTED * HALF), r] = e.astype(BF16)
+            local[half, pl.ds(b, 1), r] = top * SCALE
+            local[half, pl.ds(NB + b, 1), r] = jnp.sum(e, axis=0, keepdims=True)
+            at = lax.broadcasted_iota(jnp.int32, (HALF, CH), 0) == pos_v[pl.ds(b, 1), r] - base
+            got_here = jnp.sum(jnp.where(at, s[0:HALF], 0.0), axis=0, keepdims=True) * SCALE
+            pick[0, pl.ds(b, 1), r] = got_here if half == 0 else pick[0, pl.ds(b, 1), r] + got_here
+
+    def run(body, steps):
+        def one(n, carry):
+            body(n)
+            return carry
+
+        lax.fori_loop(0, steps, one, 0)
+
+    def passed(n):
+        hand(n, 1, (x + 2 + core) % 4 if PHASES[n][2] else (x + 1 - core) % 4, mate).wait_recv()
+        if PHASES[n][3]:
+            hand(n, 2, (x + 2 + core) % 4, mate).wait_recv()
+
     for n in range(len(PHASES)):
         for tz, ty in peers:
             o = tz * 4 + ty
-            remote(part(p_hbm.at[which(n), o], n), part(sel_v.at[which(n), o], n), d_ssem.at[n, o], d_rsem.at[n, o],
+            remote(given(which(n), o, n), kept_of(which(n), o, n), d_ssem.at[n, o], d_rsem.at[n, o],
                    device(x, core, tz, ty)).wait_recv()
-        for kind, dev in ((0, x_to), (1, mate)) if PHASES[n][2] else ((1, mate),):
+        for kind, dev in ((0, x_to), (1, mate)) if PHASES[n][3] else ((1, mate),):
             c = hand(n, kind, which(n), dev)
             c.start()
             sends.append(c)
         if n + AT_ONCE < len(PHASES):
             fetch(n + AT_ONCE)
-        if n >= 1 and PHASES[n - 1][2]:
+        if n == len(PHASES) - 2:
+            for k in range(EARLY):
+                passed(k)
+            for b in range(NB):
+                pltpu.make_async_copy(q_hbm.at[b], q_v.at[b], q_sem.at[b]).wait()
+            run(lambda b: forward(0, b), NB)
+        if n >= 1 and PHASES[n - 1][3]:
             hand_on(n - 1)
-    for n in range(len(PHASES)):
-        hand(n, 1, (x + 2 + core) % 4 if PHASES[n][1] else (x + 1 - core) % 4, mate).wait_recv()
-        if PHASES[n][2]:
-            hand(n, 2, (x + 2 + core) % 4, mate).wait_recv()
-    for b in range(NB):
-        pltpu.make_async_copy(q_hbm.at[b], q_v.at[b], q_sem.at[b]).wait()
-
-    def forward(half, k):
-        b = 2 * half + k
-        for t in range(LISTED):
-            block = tiles_ref[t, group * NB + b]
-            pq_v[b, pl.ds(t * SL, SL), :] = sel_v[block & 3, block >> 2]
-        base = (group * NB + b) * 2 * BLK + owner * SL
-        for c in range(BLK // CH):
-            r = pl.ds(c * CH, CH)
-            s = lax.dot_general(pq_v[b], q_v[b, r, :], (((1,), (1,)), ((), ())), preferred_element_type=F32)
-            top = jnp.max(s, axis=0, keepdims=True)
-            e = jnp.exp2(s * (SCALE * LOG2E) - top * (SCALE * LOG2E))
-            e_v[b, :, r] = e.astype(BF16)
-            now[half, 0, pl.ds(k, 1), r] = top * SCALE
-            now[half, 0, pl.ds(2 + k, 1), r] = jnp.sum(e, axis=0, keepdims=True)
-            at = lax.broadcasted_iota(jnp.int32, (SL, CH), 0) == pos_v[pl.ds(b, 1), r] - base
-            pick[0, pl.ds(b, 1), r] = jnp.sum(jnp.where(at, s[0:SL], 0.0), axis=0, keepdims=True) * SCALE
-
-    def run(body, steps):
-        def one(n, carry):
-            body(n)
-            return carry
-
-        lax.fori_loop(0, steps, one, 0)
+    for n in range(EARLY, len(PHASES)):
+        passed(n)
 
     spread = []
 
     def tell(half):
+        two = slice(2 * half, 2 * half + 2)
+        tot = slice(NB + 2 * half, NB + 2 * half + 2)
+        high = jnp.maximum(local[0, two], local[1, two])
+        now[half, 0, 0:2] = high
+        now[half, 0, 2:4] = sum(local[k, tot] * jnp.exp(local[k, two] - high) for k in range(2))
         for tz, ty in peers:
             c = remote(now.at[half, 0], now_buf.at[half, me], tell_ssem.at[half, tz * 4 + ty], tell_rsem.at[half, me],
                        device(x, core, tz, ty))
@@ -245,37 +275,42 @@
         now[half, 1, 0:2] = high
         now[half, 1, 2:4] = sum(p[2:4] * jnp.exp(p[0:2] - high) for p in parts)
 
-    run(lambda k: forward(0, k), 2)
+    run(lambda k: forward(1, k), 2)
     tell(0)
-    run(lambda k: forward(1, k), 2)
+    run(lambda k: forward(1, 2 + k), 2)
     tell(1)
     combine(0)
 
     def grads(half, k):
         b = 2 * half + k
         weight = ct_v[pl.ds(b, 1), :] * SCALE
-        factor = weight * jnp.exp(now[half, 0, pl.ds(k, 1), :] - now[half, 1, pl.ds(k, 1), :]) / now[half, 1, pl.ds(2 + k, 1), :]
-        base = (group * NB + b) * 2 * BLK + owner * SL
-        at = lax.broadcasted_iota(jnp.int32, (SL, BLK), 0) == pos_v[pl.ds(b, 1), :] - base
-        e_v[b, 0:SL, :] = (e_v[b, 0:SL, :].astype(F32) * factor - jnp.where(at, weight, 0.0)).astype(BF16)
-        e_v[b, SL:, :] = (e_v[b, SL:, :].astype(F32) * factor).astype(BF16)
+        for k2 in range(2):
+            factor = weight * jnp.exp(local[k2, pl.ds(b, 1), :] - now[half, 1, pl.ds(k, 1), :]) / now[half, 1, pl.ds(2 + k, 1), :]
+            base = (group * NB + b) * 2 * BLK + owner * SL + k2 * HALF
+            at = lax.broadcasted_iota(jnp.int32, (HALF, BLK), 0) == pos_v[pl.ds(b, 1), :] - base
+            one = slice(k2 * LISTED * HALF, k2 * LISTED * HALF + HALF)
+            rest = slice(k2 * LISTED * HALF + HALF, (k2 + 1) * LISTED * HALF)
+            e_v[b, one, :] = (e_v[b, one, :].astype(F32) * factor - jnp.where(at, weight, 0.0)).astype(BF16)
+            e_v[b, rest, :] = (e_v[b, rest, :].astype(F32) * factor).astype(BF16)
 
     def passage_product(b):
         out = jnp.dot(e_v[b], q_v[b], preferred_element_type=F32)
-        part_v[b, 0:LISTED] = out.astype(BF16).reshape(LISTED, SL, D)
+        part_v[b, :, 0:LISTED] = out.astype(BF16).reshape(2, LISTED, HALF, D)
 
     def query_product(b, quarter):
         r = pl.ds(pl.multiple_of(quarter * 256, 256), 256)
         out = lax.dot_general(e_v[b, :, r], pq_v[b], (((0,), (0,)), ((), ())), preferred_element_type=F32)
-        sel_v[b, pl.ds(quarter * 4, 4)] = out.astype(BF16).reshape(4, SL, D)
+        dq_v[b, pl.ds(quarter * 4, 4)] = out.astype(BF16).reshape(4, SL, D)
 
     def dense(piece, n):
         blocks = []
         for o in range(2):
             for k in range(2):
                 p = (2 * n + o) * NB + 2 * piece + k
-                blocks.append((part_v[0, slot_s[0, p]] + part_v[1, slot_s[1, p]])
-                              + (part_v[2, slot_s[2, p]] + part_v[3, slot_s[3, p]]))
+                at = [slot_s[b, p] for b in range(NB)]
+                for half in range(2):
+                    blocks.append((part_v[0, half, at[0]] + part_v[1, half, at[1]])
+                                  + (part_v[2, half, at[2]] + part_v[3, half, at[3]]))
         flat = jnp.concatenate(blocks, axis=0).T
         dp_v[piece, :, :, :, :, pl.ds(pl.multiple_of(n * 256, 256), 256)] = flat.reshape(4, 2, 2, 48, 256)
 
@@ -298,8 +333,8 @@
     z_next = [z_peers[0], z_peers[2]]
     y_next = [y_peers[0], y_peers[2]]
     left, right = pl.ds(0, 384), pl.ds(384, 384)
-    a1 = Ring(z, lambda j, h: sel_v.at[j, pl.ds(8 * h, 8), :, left], z_next, a1_buf, a1_acc, r_ssem.at[0], r_rsem.at[0])
-    b1 = Ring(y, lambda j, h: sel_v.at[pl.ds(2 * h, 2), pl.ds(4 * j, 4), :, right], y_next, b1_buf, b1_acc,
+    a1 = Ring(z, lambda j, h: dq_v.at[j, pl.ds(8 * h, 8), :, left], z_next, a1_buf, a1_acc, r_ssem.at[0], r_rsem.at[0])
+    b1 = Ring(y, lambda j, h: dq_v.at[pl.ds(2 * h, 2), pl.ds(4 * j, 4), :, right], y_next, b1_buf, b1_acc,
               r_ssem.at[1], r_rsem.at[1])
     a2 = Ring(y, lambda j, h: a1_sum.at[j, pl.ds(2 * h, 2)], y_next, a2_buf, a2_acc, r_ssem.at[2], r_rsem.at[2])
     b2 = Ring(z, lambda j, h: b1_sum.at[j, pl.ds(2 * h, 2)], z_next, b2_buf, b2_acc, r_ssem.at[3], r_rsem.at[3])
@@ -329,13 +364,11 @@
     run(both, 2)
     combine(1)
     run(lambda k: grads(1, k), 2)
-    for c in sends:
-        c.wait_send()
     opposite = (z + 2) % 4
     for c in range(3):
         r = pl.ds(c * 256, 256)
         out = lax.dot_general(e_v[opposite], pq_v[opposite, :, r], (((0,), (0,)), ((), ())), preferred_element_type=F32)
-        sel_v[opposite, :, :, r] = out.astype(BF16).reshape(16, SL, 256)
+        dq_v[opposite, :, :, r] = out.astype(BF16).reshape(16, SL, 256)
     a1.ahead()
     run(lambda n: query_product((z + 3 + n) % 4, (y + 2) % 4), 3)
     b1.ahead()
@@ -389,6 +422,10 @@
     for h in range(2):
         qg_ref[pl.ds(128 * h, 128), left] = a2.result(h).astype(BF16).reshape(128, 384)
         qg_ref[pl.ds(128 * h, 128), right] = b2.result(h).astype(BF16).reshape(128, 384)
+    keeps.append(pltpu.make_async_copy(losses_ref, losses_hbm, keep_sem.at[2]))
+    keeps.append(pltpu.make_async_copy(qg_ref, qg_hbm, keep_sem.at[3]))
+    for c in keeps[-2:]:
+        c.start()
     for piece in range(PIECES):
         for tz, ty in peers:
             n = tz * 4 + ty
@@ -396,7 +433,7 @@
                    device(x, core, tz, ty)).wait_recv()
     for moved in [picks, a1, b1, a2, b2] + xr:
         moved.drain()
-    for c in list(cores.values()) + returns + spread:
+    for c in sends + list(cores.values()) + returns + spread:
         c.wait_send()
     for c in keeps:
         c.wait()
@@ -428,17 +465,20 @@
             jax.ShapeDtypeStruct((256, D), BF16),
             jax.ShapeDtypeStruct((PIECES, 16, 96, 128), BF16),
         ],
-        in_specs=[SMEM, VMEM, VMEM, ANY, ANY],
-        out_specs=[VMEM, VMEM, ANY],
+        in_specs=[SMEM, ANY, ANY, ANY, ANY],
+        out_specs=[ANY, ANY, ANY],
         scratch_shapes=[
+            pltpu.VMEM((32, 128), jnp.int32), pltpu.VMEM((32, 128), F32),
+            pltpu.VMEM((1, 256), F32), pltpu.VMEM((256, D), BF16),
             pltpu.VMEM((NB, BLK, D), BF16),
+            pltpu.VMEM((NB, 16, HALF, D), BF16), pltpu.VMEM((NB, 16, HALF, D), BF16),
             pltpu.VMEM((NB, 16, SL, D), BF16),
             pltpu.VMEM((NB, LISTED * SL, D), BF16),
             pltpu.VMEM((NB, LISTED * SL, BLK), BF16),
-            pltpu.VMEM((NB, LISTED + 1, SL, D), BF16),
+            pltpu.VMEM((NB, 2, LISTED + 1, HALF, D), BF16),
             pltpu.VMEM((PIECES, 4, 2, 2, 48, 2048), BF16),
             pltpu.SMEM((NB, 64), jnp.int32),
-            pltpu.VMEM((8, BLK), jnp.int32), pltpu.VMEM((8, BLK), F32),
+            pltpu.VMEM((8, BLK), jnp.int32), pltpu.VMEM((8, BLK), F32), pltpu.VMEM((2, 8, BLK), F32),
             pltpu.VMEM((2, 2, 4, BLK), F32), pltpu.VMEM((2, 16, 4, BLK), F32),
             pltpu.VMEM((3, 4, BLK), F32), pltpu.VMEM((2, 3, 4, BLK), F32),
             pltpu.VMEM((2, 3, 8, SL, 384), BF16), pltpu.VMEM((2, 8, SL, 384), BF16),
@@ -450,13 +490,13 @@
             pltpu.VMEM((PIECES, 2, 3, 48, 2048), BF16), pltpu.VMEM((PIECES, 2, 48, 2048), BF16),
             pltpu.VMEM((PIECES, 4, 2, 48, 2048), BF16),
             pltpu.VMEM((PIECES, 16, 96, 128), BF16),
-            dma((NB,)), dma((2,)),
+            dma((NB,)), dma((5,)),
             dma((len(PHASES), 16)), dma((len(PHASES), 16)),
             dma((3, len(PHASES))), dma((3, len(PHASES))),
             dma((2, 3)), dma((2, 3)), dma((2, 16)), dma((2, 16)),
             dma((6, 2, 3)), dma((6, 2, 3)),
             dma((PIECES, 4)), dma((PIECES, 4)),
-            dma((PIECES, 16)), dma((PIECES, 16)), dma((PIECES,)),
+            dma((PIECES, 16)), dma((PIECES, 16)), dma((4,)),
         ],
         compiler_params=pltpu.CompilerParams(
             collective_id=1, has_side_effects=True, vmem_limit_bytes=62 * 2**20),

time: 102 us -> 99.9 us (0.979)
  Pallas kernels: 99.7 us -> 98.2 us
    pallas_call x1, Pallas kernels: 97.2 us -> 95.7 us  [whole(): pl.pallas_call(whole_kernel, out_shape=[jax.ShapeDtypeStruct((1, 256), F3...]
where the time goes in v8:
time: 99.9 us; the launch traced here: 98.8 us
  Pallas kernels  98.2 us (98%)
    pallas_call x1, Pallas kernels, whole(): pl.pallas_call(whole_kernel, out_shape=[jax.ShapeDtypeStruct((1, 256), F3...  95.7 us
    pallas_call x1, Pallas kernels, lay(): pl.pallas_call(lay_kernel, out_shape=[jax.ShapeDtypeStruct((1, 256), F32)...  2.53 us

profile of v8, /device:TPU:0, one launch (start us, length us, event | category | flops | bytes accessed | tf_op | source)
XLA Modules:
  0.0 98.8 jit_solution(12641698342068547342)
XLA Ops:
  0.6 95.7 %whole.1 = (f32[1,256]{1,0:T(1,128)}, bf16[256,768]{1,0:T(8,128)(2,1)}, bf16[2,16,96,128]{3,2,1,0:T(8,128)(2,1)}) custom-call(s32[8,32]{1,0:T(8,128)} %bitcast.11, s32[32,128]{1,0:T(8,128)} %bitcast.9, f32[32,128]{1,0:T(8,128)} %bitcast.10, bf16[4,1024,768]{2,1,0:T(8,128)(2,1)} %bitcast.7, bf16[4,16,64,768]{3,2,1,0:T(8,128)(2,1)} %bitcast.8), custom_call_target="tpu_custom_call" | custom-call | tf_op jit(solution)/shard_map/whole/pallas_call | solution.py:461
  96.3 2.5 %lay.1 = (f32[1,256]{1,0:T(1,128)}, bf16[256,768]{1,0:T(8,128)(2,1)}, bf16[96,4096]{1,0:T(8,128)(2,1)}) custom-call(f32[1,256]{1,0:T(1,128)} %get-tuple-element.9.losses_in, bf16[256,768]{1,0:T(8,128)(2,1)} %get-tuple-element.10.qg_in, bf16[2,16,96,128]{3,2,1,0:T(8,128)(2,1)} %get-tuple-element.11.got), custom_call_target="tpu_custom_call" | custom-call | tf_op jit(solution)/shard_map/lay/pallas_call | solution.py:508

commit v9 on v8

--- a/solution.py
+++ b/solution.py
@@ -375,13 +375,14 @@
     run(lambda k: passage_product(2 + k), 2)
     run(lambda n: dense(0, n), 8)
     to_core(0)
-    run(lambda n: query_product((z + 1 + 2 * (n // 3)) % 4, (y + 3 + n % 3) % 4), 6)
-    a1.raw()
+    run(lambda n: query_product((z + 1) % 4, (y + 3 + n) % 4), 3)
     add_core(0, 0)
     xr[0].ahead()
     add_core(0, 1)
     add_core(0, 2)
     xr[0].raw()
+    run(lambda n: query_product((z + 3) % 4, (y + 3 + n) % 4), 3)
+    a1.raw()
     run(lambda n: query_product(z, (y + 3 + n) % 4), 3)
     b1.raw()
     run(lambda n: dense(1, n), 8)

time: 99.9 us -> 99 us (level)
  no operation moved by 1% of the time
where the time goes in v9:
time: 99 us; the launch traced here: 98.8 us
  Pallas kernels  98.2 us (99%)
    pallas_call x1, Pallas kernels, whole(): pl.pallas_call(whole_kernel, out_shape=[jax.ShapeDtypeStruct((1, 256), F3...  95.7 us
    pallas_call x1, Pallas kernels, lay(): pl.pallas_call(lay_kernel, out_shape=[jax.ShapeDtypeStruct((1, 256), F32)...  2.53 us

profile of v9, /device:TPU:0, one launch (start us, length us, event | category | flops | bytes accessed | tf_op | source)
XLA Modules:
  0.0 98.8 jit_solution(9502768974678478086)
XLA Ops:
  0.6 95.7 %whole.1 = (f32[1,256]{1,0:T(1,128)}, bf16[256,768]{1,0:T(8,128)(2,1)}, bf16[2,16,96,128]{3,2,1,0:T(8,128)(2,1)}) custom-call(s32[8,32]{1,0:T(8,128)} %bitcast.11, s32[32,128]{1,0:T(8,128)} %bitcast.9, f32[32,128]{1,0:T(8,128)} %bitcast.10, bf16[4,1024,768]{2,1,0:T(8,128)(2,1)} %bitcast.7, bf16[4,16,64,768]{3,2,1,0:T(8,128)(2,1)} %bitcast.8), custom_call_target="tpu_custom_call" | custom-call | tf_op jit(solution)/shard_map/whole/pallas_call | solution.py:462
  96.3 2.5 %lay.1 = (f32[1,256]{1,0:T(1,128)}, bf16[256,768]{1,0:T(8,128)(2,1)}, bf16[96,4096]{1,0:T(8,128)(2,1)}) custom-call(f32[1,256]{1,0:T(1,128)} %get-tuple-element.9.losses_in, bf16[256,768]{1,0:T(8,128)(2,1)} %get-tuple-element.10.qg_in, bf16[2,16,96,128]{3,2,1,0:T(8,128)(2,1)} %get-tuple-element.11.got), custom_call_target="tpu_custom_call" | custom-call | tf_op jit(solution)/shard_map/lay/pallas_call | solution.py:509

commit v10 on v9

--- a/solution.py
+++ b/solution.py
@@ -362,6 +362,7 @@
         passage_product(k)
 
     run(both, 2)
+    run(lambda b: query_product(b, (y + 2) % 4), 2)
     combine(1)
     run(lambda k: grads(1, k), 2)
     opposite = (z + 2) % 4
@@ -370,7 +371,13 @@
         out = lax.dot_general(e_v[opposite], pq_v[opposite, :, r], (((0,), (0,)), ((), ())), preferred_element_type=F32)
         dq_v[opposite, :, :, r] = out.astype(BF16).reshape(16, SL, 256)
     a1.ahead()
-    run(lambda n: query_product((z + 3 + n) % 4, (y + 2) % 4), 3)
+
+    def late(k):
+        @pl.when(2 + k != opposite)
+        def _():
+            query_product(2 + k, (y + 2) % 4)
+
+    run(late, 2)
     b1.ahead()
     run(lambda k: passage_product(2 + k), 2)
     run(lambda n: dense(0, n), 8)

time: 99 us -> 99 us (level)
  no operation moved by 1% of the time
where the time goes in v10:
time: 99 us; the launch traced here: 98.8 us
  Pallas kernels  98.2 us (99%)
    pallas_call x1, Pallas kernels, whole(): pl.pallas_call(whole_kernel, out_shape=[jax.ShapeDtypeStruct((1, 256), F3...  95.7 us
    pallas_call x1, Pallas kernels, lay(): pl.pallas_call(lay_kernel, out_shape=[jax.ShapeDtypeStruct((1, 256), F32)...  2.53 us

profile of v10, /device:TPU:0, one launch (start us, length us, event | category | flops | bytes accessed | tf_op | source)
XLA Modules:
  0.0 98.8 jit_solution(15485992572981654165)
XLA Ops:
  0.6 95.7 %whole.1 = (f32[1,256]{1,0:T(1,128)}, bf16[256,768]{1,0:T(8,128)(2,1)}, bf16[2,16,96,128]{3,2,1,0:T(8,128)(2,1)}) custom-call(s32[8,32]{1,0:T(8,128)} %bitcast.11, s32[32,128]{1,0:T(8,128)} %bitcast.9, f32[32,128]{1,0:T(8,128)} %bitcast.10, bf16[4,1024,768]{2,1,0:T(8,128)(2,1)} %bitcast.7, bf16[4,16,64,768]{3,2,1,0:T(8,128)(2,1)} %bitcast.8), custom_call_target="tpu_custom_call" | custom-call | tf_op jit(solution)/shard_map/whole/pallas_call | solution.py:469
  96.3 2.5 %lay.1 = (f32[1,256]{1,0:T(1,128)}, bf16[256,768]{1,0:T(8,128)(2,1)}, bf16[96,4096]{1,0:T(8,128)(2,1)}) custom-call(f32[1,256]{1,0:T(1,128)} %get-tuple-element.9.losses_in, bf16[256,768]{1,0:T(8,128)(2,1)} %get-tuple-element.10.qg_in, bf16[2,16,96,128]{3,2,1,0:T(8,128)(2,1)} %get-tuple-element.11.got), custom_call_target="tpu_custom_call" | custom-call | tf_op jit(solution)/shard_map/lay/pallas_call | solution.py:516
